TPU v7x, 256 devices: a whole 4x4x8 slice. The times are simulated.
256 devices in a mesh: grp: 8 (over y, core), col: 32 (over z, x).
Axes of the slice: x: 4, y: 4, z: 8, core: 2. Of those that a mesh axis runs over, the one named last changes fastest.
Arguments:
- conductance: float32 [4, 128, 8192], P(None, 'grp', 'col'), may hold values from 0.1 to 10
- shift: float32 [128, 8192], P('grp', 'col'), may hold values from 0.05 to 1
- lanczos_vector: float32 [8, 128, 8192], P(None, 'grp', 'col'), may hold values from -6 to 6
- previous: float32 [8, 128, 8192], P(None, 'grp', 'col'), may hold values from -4 to 4
Outputs:
- next_vector: float32 [8, 128, 8192], P(None, 'grp', 'col')
- coefficients: float32 [2, 8], replicated
All inputs are finite; a program needn't handle non-finite values.
Results may differ from a plain program's by a relative error of at most 0.000043.
Values sent between devices are 32-bit elements; how exact they have to be, the bound alone decides.
A program may use at most 128 MiB of HBM per device.

v0:
```python
import jax
import jax.numpy as jnp
from jax import lax
from jax.experimental import pallas as pl
from jax.experimental.pallas import tpu as pltpu
from jax.sharding import PartitionSpec as P

F32 = jnp.float32
BF16 = jnp.bfloat16
EPSILON = 1e-06
LANES = 128
SUB = 8
ROWS = 16
COLS = 256
MESH = pl.DeviceIdType.MESH

LEVEL_ROWS = (16, 8, 4, 2)
LEVEL_PHASES = (4, 2, 2, 2)
LEVEL_STRIDE = (1, 1, 2, 4)
AROUND = ((-1, 0), (1, 0), (0, -1), (0, 1), (-1, -1), (-1, 1), (1, -1), (1, 1))
PLACE = {offset: index for index, offset in enumerate(AROUND)}


def turn_lanes(x, by):
    return pltpu.roll(x, by % LANES, 1)


def turn_strips(x, by):
    return pltpu.roll(x, by % SUB, 0)


def rows(count, body, per):
    if per >= count:
        for index in range(count):
            body(index)
    else:

        def step(index, carry):
            for inner in range(per):
                body(index * per + inner)
            return carry

        lax.fori_loop(0, count // per, step, 0)


class Grid:
    def __init__(self, rows_, phases, stride):
        self.rows, self.phases, self.stride = rows_, phases, stride

    @property
    def ghosted(self):
        return (self.rows + 2, self.phases + 2, SUB, LANES)

    @property
    def bare(self):
        return (self.rows, self.phases, SUB, LANES)

    def put(self, ref, t, r, x):
        ref[t + 1, r + 1] = x
        if r == 0:
            ref[t + 1, self.phases + 1] = turn_lanes(x, -self.stride)
        if r == self.phases - 1:
            ref[t + 1, 0] = turn_lanes(x, self.stride)

    def wrap(self, ref, colour=None):
        for r in range(-1, self.phases + 1):
            if colour is None or (self.rows - 1 + r) % 2 == colour:
                ref[0, r + 1] = turn_strips(ref[self.rows, r + 1], 1)
            if colour is None or r % 2 == colour:
                ref[self.rows + 1, r + 1] = turn_strips(ref[1, r + 1], -1)


GRIDS = tuple(Grid(*sizes) for sizes in zip(LEVEL_ROWS, LEVEL_PHASES, LEVEL_STRIDE))
DENSE = tuple(Grid(g.rows // 2, g.phases // 2, g.stride) for g in GRIDS[:3])


def level_scratch():
    shapes = []
    for index, grid in enumerate(GRIDS):
        entry = {
            "own": (4,) + grid.ghosted,
            "dia": grid.bare,
            "inv": grid.bare,
            "near": (8,) + grid.bare,
            "right": grid.ghosted,
            "red0": grid.ghosted,
            "red1": grid.ghosted,
            "black0": grid.ghosted,
            "black1": grid.ghosted,
        }
        if index < 3:
            dense = DENSE[index]
            entry["weights"] = (8,) + dense.ghosted
            entry["passed"] = (6,) + dense.ghosted
            entry["kept"] = (5,) + dense.bare
            entry["residual"] = grid.ghosted
            entry["lifted"] = dense.ghosted
        shapes.append({name: pltpu.VMEM(shape, F32) for name, shape in entry.items()})
    return shapes


class Level:
    def __init__(self, index, refs, per):
        self.index, self.grid, self.per = index, GRIDS[index], per
        for name, ref in refs.items():
            setattr(self, name, ref)
        self.buffers = ((self.red0, self.red1), (self.black0, self.black1))
        self.now = [self.right, None]

    def pairs(self, body):
        rows(self.grid.rows // 2, body, self.per)

    def edge(self, a, b, t, r):
        own = self.own
        if (a, b) == (0, 1):
            return own[0, t + 1, r + 1]
        if (a, b) == (0, -1):
            return own[0, t + 1, r]
        if (a, b) == (1, 0):
            return own[1, t + 1, r + 1]
        if (a, b) == (-1, 0):
            return own[1, t, r + 1]
        if (a, b) == (1, 1):
            return own[2, t + 1, r + 1]
        if (a, b) == (-1, -1):
            return own[2, t, r]
        if (a, b) == (1, -1):
            return own[3, t + 1, r + 1]
        return own[3, t, r + 2]

    def scale_edges(self, t, r, edges, diagonal):
        inverse = 1.0 / diagonal
        self.dia[t, r] = diagonal
        self.inv[t, r] = inverse
        for index, edge in enumerate(edges):
            self.near[index, t, r] = edge * inverse

    def gathered(self, t, r, offsets, source, start=None):
        terms = [
            self.near[PLACE[a, b], t, r] * source(a, b)[t + 1 + a, r + 1 + b] for a, b in offsets
        ]
        if start is not None:
            terms.append(start)
        while len(terms) > 1:
            terms = [
                terms[i] + terms[i + 1] if i + 1 < len(terms) else terms[i]
                for i in range(0, len(terms), 2)
            ]
        return terms[0]

    def spare(self, colour):
        first, second = self.buffers[colour]
        return second if self.now[colour] is first else first

    def half_sweep(self, colour):
        grid, other, same = self.grid, self.now[1 - colour], self.now[colour]
        out = self.spare(colour)
        offsets = AROUND if same is not None else AROUND[:4]

        def body(u):
            for odd in (0, 1):
                for r in range(grid.phases):
                    if (odd + r) % 2 == colour:
                        t = 2 * u + odd
                        x = self.gathered(
                            t,
                            r,
                            offsets,
                            lambda a, b: other if (a + b) % 2 else same,
                            self.right[t + 1, r + 1],
                        )
                        grid.put(out, t, r, x)

        self.pairs(body)
        grid.wrap(out, colour)
        self.now[colour] = out

    def smooth_from_zero(self):
        self.now = [self.right, None]
        for colour in (1, 0, 1):
            self.half_sweep(colour)

    def smooth(self):
        for colour in (0, 1, 0, 1):
            self.half_sweep(colour)

    def find_residual(self):
        grid = self.grid

        def body(u):
            for odd in (0, 1):
                for r in range(grid.phases):
                    t = 2 * u + odd
                    colour = (odd + r) % 2
                    x = self.gathered(
                        t,
                        r,
                        AROUND,
                        lambda a, b: self.now[(colour + a + b) % 2],
                        self.right[t + 1, r + 1] - self.now[colour][t + 1, r + 1],
                    )
                    grid.put(self.residual, t, r, self.dia[t, r] * x)

        self.pairs(body)
        grid.wrap(self.residual)

    def find_weights(self):
        grid, dense, edge = self.grid, DENSE[self.index], self.edge

        def edges(i):
            for p in range(dense.phases):
                t, r = 2 * i + 1, 2 * p
                middle = 1.0 / (self.dia[t, r] - edge(0, -1, t, r) - edge(0, 1, t, r))
                up = edge(-1, 0, t, r) + edge(-1, -1, t, r) + edge(-1, 1, t, r)
                down = edge(1, 0, t, r) + edge(1, -1, t, r) + edge(1, 1, t, r)
                dense.put(self.weights.at[0], i, p, up * middle)
                dense.put(self.weights.at[1], i, p, down * middle)
                t, r = 2 * i, 2 * p + 1
                middle = 1.0 / (self.dia[t, r] - edge(-1, 0, t, r) - edge(1, 0, t, r))
                left = edge(0, -1, t, r) + edge(-1, -1, t, r) + edge(1, -1, t, r)
                right = edge(0, 1, t, r) + edge(-1, 1, t, r) + edge(1, 1, t, r)
                dense.put(self.weights.at[2], i, p, left * middle)
                dense.put(self.weights.at[3], i, p, right * middle)

        rows(dense.rows, edges, self.per)
        for index in range(4):
            dense.wrap(self.weights.at[index])
        w = self.weight

        def corners(i):
            for p in range(dense.phases):
                n = lambda a, b: self.near[PLACE[a, b], 2 * i + 1, 2 * p + 1]
                here = n(-1, -1) + n(0, -1) * w(0, i, p) + n(-1, 0) * w(2, i, p)
                down = n(1, -1) + n(0, -1) * w(1, i, p) + n(1, 0) * w(2, i + 1, p)
                right = n(-1, 1) + n(0, 1) * w(0, i, p + 1) + n(-1, 0) * w(3, i, p)
                both = n(1, 1) + n(0, 1) * w(1, i, p + 1) + n(1, 0) * w(3, i + 1, p)
                for index, x in enumerate((here, down, right, both)):
                    dense.put(self.weights.at[4 + index], i, p, x)

        rows(dense.rows, corners, self.per)
        for index in range(4, 8):
            dense.wrap(self.weights.at[index])

    def weight(self, index, i, p):
        return self.weights[index, i + 1, p + 1]

    def find_product(self):
        dense, w = DENSE[self.index], self.weight
        up, down, left, right, here, below, beside, both = range(8)

        def body(i):
            for p in range(dense.phases):
                t, r = 2 * i, 2 * p
                c = lambda a, b: self.edge(a, b, t, r)
                center = (
                    self.dia[t, r]
                    - c(-1, 0) * w(down, i - 1, p)
                    - c(1, 0) * w(up, i, p)
                    - c(0, -1) * w(right, i, p - 1)
                    - c(0, 1) * w(left, i, p)
                ) - (
                    c(-1, -1) * w(both, i - 1, p - 1)
                    + c(-1, 1) * w(below, i - 1, p)
                    + c(1, -1) * w(beside, i, p - 1)
                    + c(1, 1) * w(here, i, p)
                )
                east = -(
                    c(0, 1) * w(right, i, p)
                    + c(-1, 1) * w(both, i - 1, p)
                    + c(1, 1) * w(beside, i, p)
                )
                south = -(
                    c(1, 0) * w(down, i, p)
                    + c(1, 1) * w(below, i, p)
                    + c(1, -1) * w(both, i, p - 1)
                )
                south_east = -c(1, 1) * w(both, i, p)
                south_west = -c(1, -1) * w(below, i, p - 1)
                t, r = 2 * i + 1, 2 * p
                v = lambda a, b: self.edge(a, b, t, r)
                d = self.dia[t, r]
                v00 = (
                    d * w(up, i, p)
                    - v(-1, 0)
                    - v(-1, -1) * w(right, i, p - 1)
                    - v(-1, 1) * w(left, i, p)
                    - v(0, -1) * w(beside, i, p - 1)
                    - v(0, 1) * w(here, i, p)
                )
                v10 = (
                    d * w(down, i, p)
                    - v(1, 0)
                    - v(1, -1) * w(right, i + 1, p - 1)
                    - v(1, 1) * w(left, i + 1, p)
                    - v(0, -1) * w(both, i, p - 1)
                    - v(0, 1) * w(below, i, p)
                )
                v01 = -v(-1, 1) * w(right, i, p) - v(0, 1) * w(beside, i, p)
                v11 = -v(1, 1) * w(right, i + 1, p) - v(0, 1) * w(both, i, p)
                v1m = -v(1, -1) * w(left, i + 1, p - 1) - v(0, -1) * w(below, i, p - 1)
                t, r = 2 * i, 2 * p + 1
                h = lambda a, b: self.edge(a, b, t, r)
                d = self.dia[t, r]
                h00 = (
                    d * w(left, i, p)
                    - h(0, -1)
                    - h(-1, -1) * w(down, i - 1, p)
                    - h(1, -1) * w(up, i, p)
                    - h(-1, 0) * w(below, i - 1, p)
                    - h(1, 0) * w(here, i, p)
                )
                h01 = (
                    d * w(right, i, p)
                    - h(0, 1)
                    - h(-1, 1) * w(down, i - 1, p + 1)
                    - h(1, 1) * w(up, i, p + 1)
                    - h(-1, 0) * w(both, i - 1, p)
                    - h(1, 0) * w(beside, i, p)
                )
                h10 = -h(1, -1) * w(down, i, p) - h(1, 0) * w(below, i, p)
                h11 = -h(1, 1) * w(down, i, p + 1) - h(1, 0) * w(both, i, p)
                t, r = 2 * i + 1, 2 * p + 1
                k = lambda a, b: self.edge(a, b, t, r)
                d = self.dia[t, r]
                k00 = (
                    d * w(here, i, p)
                    - k(-1, -1)
                    - k(-1, 0) * w(left, i, p)
                    - k(0, -1) * w(up, i, p)
                )
                k10 = (
                    d * w(below, i, p)
                    - k(1, -1)
                    - k(1, 0) * w(left, i + 1, p)
                    - k(0, -1) * w(down, i, p)
                )
                k01 = (
                    d * w(beside, i, p)
                    - k(-1, 1)
                    - k(-1, 0) * w(right, i, p)
                    - k(0, 1) * w(up, i, p + 1)
                )
                k11 = (
                    d * w(both, i, p)
                    - k(1, 1)
                    - k(1, 0) * w(right, i + 1, p)
                    - k(0, 1) * w(down, i, p + 1)
                )
                wu, wd, wl, wr = (w(index, i, p) for index in (up, down, left, right))
                ch, cd, cr, cb = (w(index, i, p) for index in (here, below, beside, both))
                self.kept[0, i, p] = center + (wu * v00 + wl * h00) + ch * k00
                self.kept[1, i, p] = east + (wu * v01 + wl * h01) + ch * k01
                self.kept[2, i, p] = south + (wu * v10 + wl * h10) + ch * k10
                self.kept[3, i, p] = south_east + (wu * v11 + wl * h11) + ch * k11
                self.kept[4, i, p] = south_west + wu * v1m
                passed = (
                    wd * v10 + cd * k10,
                    wd * v11 + cd * k11,
                    wr * h01 + cr * k01,
                    wr * h11 + cr * k11,
                    wr * h10 + cr * k10,
                    cb * k11,
                )
                for index, x in enumerate(passed):
                    dense.put(self.passed.at[index], i, p, x)

        rows(dense.rows, body, self.per)
        for index in range(6):
            dense.wrap(self.passed.at[index])

    def give_product(self, coarse):
        dense, grid = DENSE[self.index], coarse.grid

        def body(i):
            for p in range(dense.phases):
                sent = lambda index, di, dp: self.passed[index, i + 1 + di, p + 1 + dp]
                center = (
                    self.kept[0, i, p] + sent(0, -1, 0) + sent(2, 0, -1) + sent(5, -1, -1)
                )
                entries = (
                    self.kept[1, i, p] + sent(1, -1, 0),
                    self.kept[2, i, p] + sent(3, 0, -1),
                    self.kept[3, i, p],
                    self.kept[4, i, p] + sent(4, 0, -1),
                )
                for phase, by in coarse.places(p, dense):
                    coarse.dia[i, phase] = center if by == 0 else turn_lanes(center, by)
                    for index, x in enumerate(entries):
                        x = -x if by == 0 else turn_lanes(-x, by)
                        grid.put(coarse.own.at[index], i, phase, x)

        rows(dense.rows, body, coarse.per)
        for index in range(4):
            grid.wrap(coarse.own.at[index])

        def scaled(u):
            for odd in (0, 1):
                for r in range(grid.phases):
                    t = 2 * u + odd
                    coarse.scale_edges(
                        t, r, [coarse.edge(a, b, t, r) for a, b in AROUND], coarse.dia[t, r]
                    )

        coarse.pairs(scaled)

    def places(self, p, dense):
        if dense.phases == self.grid.phases:
            return ((p, 0),)
        return ((0, 0), (1, -dense.stride))

    def restrict(self, coarse):
        dense, w, res = DENSE[self.index], self.weight, self.residual

        def body(i):
            for p in range(dense.phases):
                f = lambda a, b: res[2 * i + a + 1, 2 * p + b + 1]
                x = (
                    (f(0, 0) + w(0, i, p) * f(1, 0))
                    + (w(1, i - 1, p) * f(-1, 0) + w(2, i, p) * f(0, 1))
                ) + (
                    (w(3, i, p - 1) * f(0, -1) + w(4, i, p) * f(1, 1))
                    + (
                        (w(5, i - 1, p) * f(-1, 1) + w(6, i, p - 1) * f(1, -1))
                        + w(7, i - 1, p - 1) * f(-1, -1)
                    )
                )
                for phase, by in coarse.places(p, dense):
                    y = x if by == 0 else turn_lanes(x, by)
                    coarse.grid.put(coarse.right, i, phase, y * coarse.inv[i, phase])

        rows(dense.rows, body, coarse.per)
        coarse.grid.wrap(coarse.right)

    def prolong(self, coarse):
        grid, dense, w = self.grid, DENSE[self.index], self.weight
        if dense.phases == coarse.grid.phases:
            e = lambda i, p, parity: coarse.now[parity % 2][i + 1, p + 1]
        else:
            lane = lax.broadcasted_iota(jnp.int32, (SUB, LANES), 1)
            even = (lane & dense.stride) == 0
            for i in range(dense.rows):
                first = coarse.now[i % 2][i + 1, 1]
                second = turn_lanes(coarse.now[(i + 1) % 2][i + 1, 2], dense.stride)
                dense.put(self.lifted, i, 0, jnp.where(even, first, second))
            dense.wrap(self.lifted)
            e = lambda i, p, parity: self.lifted[i + 1, p + 1]
        outs = [self.spare(0), self.spare(1)]

        def body(v):
            for odd in (0, 1):
                i = 2 * v + odd
                for p in range(dense.phases):
                    here = e(i, p, odd + p)
                    below = e(i + 1, p, odd + p + 1)
                    beside = e(i, p + 1, odd + p + 1)
                    both = e(i + 1, p + 1, odd + p)
                    changes = (
                        (0, 0, here),
                        (1, 0, w(0, i, p) * here + w(1, i, p) * below),
                        (0, 1, w(2, i, p) * here + w(3, i, p) * beside),
                        (
                            1,
                            1,
                            (w(4, i, p) * here + w(5, i, p) * below)
                            + (w(6, i, p) * beside + w(7, i, p) * both),
                        ),
                    )
                    for a, b, change in changes:
                        colour = (a + b) % 2
                        t, r = 2 * i + a, 2 * p + b
                        grid.put(outs[colour], t, r, self.now[colour][t + 1, r + 1] + change)

        rows(dense.rows // 2, body, self.per)
        for colour in (0, 1):
            grid.wrap(outs[colour], colour)
            self.now[colour] = outs[colour]


def reorder(x, order):
    high = x.astype(BF16)
    rest = x - high.astype(F32)
    middle = rest.astype(BF16)
    low = (rest - middle.astype(F32)).astype(BF16)
    moved = [jnp.dot(part, order, preferred_element_type=F32) for part in (low, middle, high)]
    return (moved[0] + moved[1]) + moved[2]


def phase_matrix(swap, inverse):
    natural = lax.broadcasted_iota(jnp.int32, (COLS, COLS), 1 if inverse else 0)
    phased = lax.broadcasted_iota(jnp.int32, (COLS, COLS), 0 if inverse else 1)
    phase = natural & 3
    if swap:
        phase = phase ^ 1
    target = phase * 64 + (natural >> 2)
    return jnp.where(phased == target, 1.0, 0.0).astype(BF16)


def spread(field, own, halo, own_order, halo_order, own_out, halo_out):
    for out, x in ((own_out, reorder(own, own_order)), (halo_out, reorder(halo, halo_order))):
        for pair in (0, 1):
            out[field, pair] = x[:, pair * LANES : (pair + 1) * LANES]


def phases_of(field, t, own_out, halo_out, low):
    found = []
    for pair in (0, 1):
        window = (pl.ds(t, SUB, stride=ROWS), slice(None))
        own, halo = own_out.at[field, pair][window], halo_out.at[field, pair][window]
        found.append(jnp.where(low, own, halo))
        found.append(turn_lanes(jnp.where(low, halo, own), 64))
    return found


def fill_edges(level, col_place, own_out, halo_out):
    grid = level.grid
    lane = lax.broadcasted_iota(jnp.int32, (SUB, LANES), 1)
    strip = lax.broadcasted_iota(jnp.int32, (SUB, LANES), 0)
    low = lane < 64
    lane_start = col_place * 64 + jnp.where(lane < 96, lane, lane - LANES)
    count = lax.axis_size("col") * 64
    east_ok = jnp.where((lane_start == count - 1) | (lane_start == -1), 0.0, 1.0)
    west_ok = jnp.where((lane_start == 0) | (lane_start == count), 0.0, 1.0)
    last_strip = strip == SUB - 1

    def body(t):
        south_ok = jnp.where(last_strip & (t == ROWS - 1), 0.0, 1.0)
        for index in range(4):
            phases = phases_of(index, t, own_out, halo_out, low)
            for r, x in enumerate(phases):
                if index != 0:
                    x = x * south_ok
                if index in (0, 2) and r == 3:
                    x = x * east_ok
                if index == 3 and r == 0:
                    x = x * west_ok
                grid.put(level.own.at[index], t, r, x)

    rows(ROWS, body, 2)
    for index in range(4):
        grid.wrap(level.own.at[index])

    def scaled(t):
        shift = phases_of(4, t, own_out, halo_out, low)
        for r in range(4):
            edges = [level.edge(a, b, t, r) for a, b in AROUND]
            pairs = [edges[i] + edges[i + 1] for i in range(0, 8, 2)]
            total = (pairs[0] + pairs[1]) + (pairs[2] + pairs[3])
            level.scale_edges(t, r, edges, shift[r] + total)

    rows(ROWS, scaled, 2)


def fill_right(level, own_out, halo_out):
    grid = level.grid
    vector = level.residual
    lane = lax.broadcasted_iota(jnp.int32, (SUB, LANES), 1)
    low = lane < 64

    def body(t):
        for r, x in enumerate(phases_of(5, t, own_out, halo_out, low)):
            grid.put(vector, t, r, x)

    rows(ROWS, body, 4)
    grid.wrap(vector)

    def image(u):
        for odd in (0, 1):
            for r in range(4):
                t = 2 * u + odd
                x = vector[t + 1, r + 1] - level.gathered(t, r, AROUND, lambda a, b: vector)
                grid.put(level.right, t, r, x)

    level.pairs(image)
    grid.wrap(level.right)


def setup(levels):
    for index in range(3):
        levels[index].find_weights()
        levels[index].find_product()
        levels[index].give_product(levels[index + 1])


def cycle(levels, index):
    level = levels[index]
    level.smooth_from_zero()
    if index == 3:
        return
    level.find_residual()
    level.restrict(levels[index + 1])
    cycle(levels, index + 1)
    level.prolong(levels[index + 1])
    level.smooth()


def total(x):
    return jnp.sum(jnp.sum(x, axis=0, keepdims=True), axis=1, keepdims=True)


def tell(solved, vector, previous):
    target = solved - previous
    length = total(vector * vector)
    projected = total(vector * target)
    near_alpha = jnp.where(length > 0.0, projected / jnp.where(length > 0.0, length, 1.0), 0.0)
    rest = target - near_alpha * vector
    squares = total(rest * rest)
    cross = total(vector * rest)
    inner = total(vector * solved)
    lane = lax.broadcasted_iota(jnp.int32, (1, LANES), 1)
    row = jnp.where(lane < 3, near_alpha, 0.0)
    for place, x in ((3, inner), (64, squares), (65, cross), (66, length)):
        row = jnp.where(lane == place, x, row)
    return row


def conclude(told, cells):
    lane = lax.broadcasted_iota(jnp.int32, told.shape, 1)
    alpha = total(jnp.where(lane == 3, told, 0.0)) / cells
    delta = alpha - told
    sums = pltpu.roll(told, 64, 1)
    weight = jnp.where(lane == 0, 1.0, jnp.where(lane == 1, -2.0 * delta, delta * delta))
    squares = total(jnp.where(lane < 3, weight * sums, 0.0)) / cells
    scale = jnp.sqrt(jnp.maximum(squares, 0.0) + EPSILON)
    return alpha, scale


def compute(col_place, own, halo, vector, vector_halo, previous, solved, told, levels_refs, own_out, halo_out, phased):
    levels = [Level(index, refs, 2 if index == 0 else 99) for index, refs in enumerate(levels_refs)]
    own_order = phase_matrix(False, False)
    halo_order = phase_matrix(True, False)
    whole = (SUB * ROWS, COLS)
    half = (SUB * ROWS, LANES)
    for field in range(5):
        sides = [halo[:, side, field].reshape(half) for side in (0, 1)]
        spread(
            field,
            own[:, field].reshape(whole),
            jnp.concatenate(sides, axis=1),
            own_order,
            halo_order,
            own_out,
            halo_out,
        )
    sides = [vector_halo[side].reshape(half) for side in (0, 1)]
    spread(
        5,
        vector[...].reshape(whole),
        jnp.concatenate(sides, axis=1),
        own_order,
        halo_order,
        own_out,
        halo_out,
    )
    fill_edges(levels[0], col_place, own_out, halo_out)
    fill_right(levels[0], own_out, halo_out)
    setup(levels)
    cycle(levels, 0)
    lane = lax.broadcasted_iota(jnp.int32, (SUB, LANES), 1)
    low = lane < 64

    def gather(u):
        for odd in (0, 1):
            t = 2 * u + odd
            x = [levels[0].now[(odd + r) % 2][t + 1, r + 1] for r in range(4)]
            for pair in (0, 1):
                y = jnp.where(low, x[2 * pair], turn_lanes(x[2 * pair + 1], 64))
                phased.at[pair][pl.ds(t, SUB, stride=ROWS), :] = y

    rows(ROWS // 2, gather, 2)
    result = reorder(jnp.concatenate([phased[0], phased[1]], axis=1), phase_matrix(False, True))
    solved[...] = result.reshape(SUB, ROWS, COLS)
    told[...] = tell(result, vector[...].reshape(whole), previous[...].reshape(whole))


def copy_out(source, target, send, receive, grp, col):
    return pltpu.make_async_remote_copy(
        src_ref=source,
        dst_ref=target,
        send_sem=send,
        recv_sem=receive,
        device_id=(grp, col),
        device_id_type=MESH,
    )


def greet(partners):
    barrier = pltpu.get_barrier_semaphore()
    for grp, col in partners:
        pl.semaphore_signal(barrier, inc=1, device_id=(grp, col), device_id_type=MESH)
    pl.semaphore_wait(barrier, len(partners))


def gather_semaphores():
    dma = pltpu.SemaphoreType.DMA
    return [dma((2, 3)), dma((2, 7)), dma((2, 7)), dma((2, 8)), dma((2, 2)), dma((2, 4)), dma((2, 8))]


def gather_sources(g, conductance, shift, vector_in, previous_in, own, vector, previous):
    own[g, 0:4] = conductance[...]
    own[g, 4] = shift[...]
    vector[g] = vector_in[g]
    previous[g] = previous_in[g]


def gather(g, c, vector_in, previous_in, own, halo, vector, vector_halo, previous, semaphores):
    along, of_vector, of_previous, beside, vector_beside, across, halo_across = semaphores
    n_grp, n_col = 8, lax.axis_size("col")
    y, core = g // 2, g % 2
    twin = y * 2 + 1 - core
    mates = [(g + step) % n_grp for step in range(1, n_grp)]
    east, west = (c + 1) % n_col, (c + n_col - 1) % n_col
    started = []

    def start(copy):
        copy.start()
        started.append(copy)
        return copy

    def place(back):
        return ((y + 4 - back) % 4) * 2 + core

    def send_sides(back):
        rows_ = place(back)
        return [
            start(
                copy_out(
                    own.at[rows_, :, :, pl.ds(LANES, LANES)],
                    halo.at[rows_, 1],
                    beside.at[0, back],
                    beside.at[1, back],
                    g,
                    east,
                )
            ),
            start(
                copy_out(
                    own.at[rows_, :, :, pl.ds(0, LANES)],
                    halo.at[rows_, 0],
                    beside.at[0, 4 + back],
                    beside.at[1, 4 + back],
                    g,
                    west,
                )
            ),
        ]

    def send_across(back):
        rows_ = place(back)
        return start(
            copy_out(own.at[rows_], own.at[rows_], across.at[0, back], across.at[1, back], twin, c)
        )

    arriving = []
    for step in range(1, 4):
        to = ((y + step) % 4) * 2 + core
        arriving.append(
            start(
                copy_out(own.at[g], own.at[g], along.at[0, step - 1], along.at[1, step - 1], to, c)
            )
        )
    from_sides = [send_sides(0)]
    from_twin = [send_across(0)]
    vectors = [
        start(
            copy_out(
                vector_in.at[to], vector.at[g], of_vector.at[0, i], of_vector.at[1, i], to, c
            )
        )
        for i, to in enumerate(mates)
    ]
    for back in (1, 3, 2):
        arriving[back - 1].wait_recv()
        from_sides.append(send_sides(back))
        from_twin.append(send_across(back))
    for copy in vectors:
        copy.wait_recv()
    side_vectors = []
    for side, to in ((1, east), (0, west)):
        side_vectors.append(
            start(
                copy_out(
                    vector.at[:, :, pl.ds(side * LANES, LANES)],
                    vector_halo.at[side],
                    vector_beside.at[0, side],
                    vector_beside.at[1, side],
                    g,
                    to,
                )
            )
        )
    previouses = [
        start(
            copy_out(
                previous_in.at[to],
                previous.at[g],
                of_previous.at[0, i],
                of_previous.at[1, i],
                to,
                c,
            )
        )
        for i, to in enumerate(mates)
    ]
    halves = []
    for order, back in enumerate((0, 1, 3, 2)):
        for side in (1, 0):
            from_sides[order][1 - side].wait_recv()
            rows_ = place(back)
            at = side * 4 + back
            halves.append(
                start(
                    copy_out(
                        halo.at[rows_, side],
                        halo.at[rows_, side],
                        halo_across.at[0, at],
                        halo_across.at[1, at],
                        twin,
                        c,
                    )
                )
            )
    for copy in from_twin + halves + side_vectors:
        copy.wait_recv()

    def finish():
        for copy in previouses:
            copy.wait_recv()
        for copy in started:
            copy.wait_send()

    return finish


def finish_semaphores():
    dma = pltpu.SemaphoreType.DMA
    return [dma((2,)), dma((2, 7)), dma((2,))]


def finish_scratch(n_col):
    return [
        pltpu.VMEM((8, ROWS, COLS), F32),
        pltpu.VMEM((n_col, 1, LANES), F32),
        pltpu.VMEM((8, 2, LANES), F32),
    ]


def conclude_all(g, c, vector_in, previous_in, solved, told, got, heard, verdicts, out, coefficients, semaphores):
    spread_sem, back_sem, verdict_sem = semaphores
    n_grp, n_col = 8, lax.axis_size("col")
    mates = [(g + step) % n_grp for step in range(1, n_grp)]
    heard[c] = told[...]
    telling = []
    for step in range(1, n_col):
        to = (c + step) % n_col
        telling.append(copy_out(told, heard.at[c], spread_sem.at[0], spread_sem.at[1], g, to))
        telling[-1].start()
    back = []
    for i, to in enumerate(mates):
        back.append(copy_out(solved.at[to], got.at[g], back_sem.at[0, i], back_sem.at[1, i], to, c))
        back[-1].start()
    got[g] = solved[g]
    several = heard.at[pl.ds(0, n_col - 1)]
    pltpu.make_async_copy(several, several, spread_sem.at[1]).wait()
    alpha, scale = conclude(heard[...].reshape(n_col, LANES), float(n_grp * ROWS * n_col * COLS))
    which = lax.broadcasted_iota(jnp.int32, (2, LANES), 0)
    verdicts[g] = jnp.where(which == 0, alpha, scale)
    deciding = []
    for to in mates:
        deciding.append(
            copy_out(verdicts.at[g], verdicts.at[g], verdict_sem.at[0], verdict_sem.at[1], to, c)
        )
        deciding[-1].start()
    for copy in back:
        copy.wait_recv()
    others = verdicts.at[pl.ds(0, n_grp - 1)]
    pltpu.make_async_copy(others, others, verdict_sem.at[1]).wait()
    lane = lax.broadcasted_iota(jnp.int32, (2, LANES), 1)
    summary = jnp.zeros((2, LANES), F32)
    for probe in range(n_grp):
        pair = verdicts[probe]
        summary = jnp.where(lane == probe, pair, summary)
        rest = got[probe] - pair[0:1, 0:1] * vector_in[probe] - previous_in[probe]
        out[probe] = rest * (1.0 / pair[1:2, 0:1])
    coefficients[...] = summary[:, 0:n_grp]
    pltpu.make_async_copy(several, several, spread_sem.at[0]).wait()
    pltpu.make_async_copy(others, others, verdict_sem.at[0]).wait()
    for copy in back:
        copy.wait_send()


def flat_levels():
    return jax.tree.flatten(level_scratch())


def spread_scratch():
    return [pltpu.VMEM((6, 2, 8 * ROWS, LANES), F32)] * 2 + [pltpu.VMEM((2, 8 * ROWS, LANES), F32)]


VMEM = pl.BlockSpec(memory_space=pltpu.VMEM)
LIMIT = 48 * 1024 * 1024


def shape(*dims):
    return jax.ShapeDtypeStruct(dims, F32)


def gather_kernel(conductance, shift, vector_in, previous_in, own, halo, vector, vector_halo, previous, *semaphores):
    g, c = lax.axis_index("grp"), lax.axis_index("col")
    n_col = lax.axis_size("col")
    gather_sources(g, conductance, shift, vector_in, previous_in, own, vector, previous)
    greet(
        [((g + step) % 8, c) for step in range(1, 8)]
        + [(g, (c + 1) % n_col), (g, (c + n_col - 1) % n_col)]
    )
    gather(g, c, vector_in, previous_in, own, halo, vector, vector_halo, previous, semaphores)()


def compute_kernel(own, halo, vector, vector_halo, previous, solved, told, *scratch):
    leaves, tree = flat_levels()
    count = len(leaves)
    levels_refs = jax.tree.unflatten(tree, scratch[:count])
    own_out, halo_out, phased = scratch[count:]
    c = lax.axis_index("col")
    compute(c, own, halo, vector, vector_halo, previous, solved, told, levels_refs, own_out, halo_out, phased)


def finish_kernel(vector_in, previous_in, solved, told, out, coefficients, got, heard, verdicts, *semaphores):
    g, c = lax.axis_index("grp"), lax.axis_index("col")
    n_col = lax.axis_size("col")
    greet(
        [((g + step) % 8, c) for step in range(1, 8)]
        + [(g, (c + step) % n_col) for step in range(1, n_col)]
    )
    conclude_all(g, c, vector_in, previous_in, solved, told, got, heard, verdicts, out, coefficients, semaphores)


def local(conductance, shift, vector_in, previous_in):
    n_col = lax.axis_size("col")
    gathered = pl.pallas_call(
        gather_kernel,
        out_shape=(
            shape(8, 5, ROWS, COLS),
            shape(8, 2, 5, ROWS, LANES),
            shape(8, ROWS, COLS),
            shape(2, 8, ROWS, LANES),
            shape(8, ROWS, COLS),
        ),
        in_specs=[VMEM] * 4,
        out_specs=(VMEM,) * 5,
        scratch_shapes=gather_semaphores(),
        compiler_params=pltpu.CompilerParams(collective_id=0, has_side_effects=True, vmem_limit_bytes=LIMIT),
    )(conductance, shift, vector_in, previous_in)
    leaves, _ = flat_levels()
    solved, told = pl.pallas_call(
        compute_kernel,
        out_shape=(shape(8, ROWS, COLS), shape(1, LANES)),
        in_specs=[VMEM] * 5,
        out_specs=(VMEM,) * 2,
        scratch_shapes=leaves + spread_scratch(),
        compiler_params=pltpu.CompilerParams(vmem_limit_bytes=LIMIT),
    )(*gathered)
    return pl.pallas_call(
        finish_kernel,
        out_shape=(shape(8, ROWS, COLS), shape(2, 8)),
        in_specs=[VMEM] * 4,
        out_specs=(VMEM,) * 2,
        scratch_shapes=finish_scratch(n_col) + finish_semaphores(),
        compiler_params=pltpu.CompilerParams(collective_id=1, has_side_effects=True, vmem_limit_bytes=LIMIT),
    )(vector_in, previous_in, solved, told)


def solution(mesh):
    in_specs = (
        P(None, "grp", "col"),
        P("grp", "col"),
        P(None, "grp", "col"),
        P(None, "grp", "col"),
    )
    out_specs = (P(None, "grp", "col"), P())
    return jax.shard_map(local, mesh=mesh, in_specs=in_specs, out_specs=out_specs, check_vma=False)
```

profile of v0, /device:TPU:1, one launch (start us, length us, event | category | flops | bytes accessed | tf_op | source)
XLA Modules:
  0.0 55.2 jit_solution(13519897459347018225)
XLA Ops:
  0.6 0.0 copy-start
  0.6 0.9 %copy-done = f32[8,16,256]{2,1,0:T(8,128)S(1)} copy-done((f32[8,16,256]{2,1,0:T(8,128)S(1)}, f32[8,16,256]{2,1,0:T(8,128)}, u32[]{:S(2)}) %copy-start) | copy-done | bytes 131096
  1.5 0.0 copy-start.2
  1.5 0.9 %copy-done.2 = f32[8,16,256]{2,1,0:T(8,128)S(1)} copy-done((f32[8,16,256]{2,1,0:T(8,128)S(1)}, f32[8,16,256]{2,1,0:T(8,128)}, u32[]{:S(2)}) %copy-start.2) | copy-done | bytes 131096
  2.4 0.0 copy-start.4
  2.4 0.8 %copy-done.4 = f32[4,16,256]{2,1,0:T(8,128)S(1)} copy-done((f32[4,16,256]{2,1,0:T(8,128)S(1)}, f32[4,16,256]{2,1,0:T(8,128)}, u32[]{:S(2)}) %copy-start.4) | copy-done | bytes 65560
  3.3 0.0 copy-start.5
  3.3 0.7 %copy-done.5 = f32[16,256]{1,0:T(8,128)S(1)} copy-done((f32[16,256]{1,0:T(8,128)S(1)}, f32[16,256]{1,0:T(8,128)}, u32[]{:S(2)}) %copy-start.5) | copy-done | bytes 16408
  4.0 23.0 %shard_map.59 = (f32[8,5,16,256]{3,2,1,0:T(8,128)S(1)}, f32[8,2,5,16,128]{4,3,2,1,0:T(8,128)S(1)}, f32[8,16,256]{2,1,0:T(8,128)S(1)}, f32[2,8,16,128]{3,2,1,0:T(8,128)S(1)}, f32[8,16,256]{2,1,0:T(8,128)S(1)}) custom-call(f32[4,16,256]{2,1,0:T(8,128)S(1)} %copy-done.4, f32[16,256]{1,0:T(8,128)S(1)} %copy-done.5, f32[8,16,256]{2,1,0:T(8,128)S(1)} %copy-done, ...), custom_call_target="tpu_custom_call" | custom-call | tf_op jit(solution)/shard_map/pallas_call | solution.py:939
  27.0 0.0 copy-start.1
  27.0 0.0 copy-start.3
  27.0 12.1 %shard_map.60 = (f32[8,16,256]{2,1,0:T(8,128)S(1)}, f32[1,128]{1,0:T(1,128)S(1)}) custom-call(f32[8,5,16,256]{3,2,1,0:T(8,128)S(1)} %get-tuple-element.9.own, f32[8,2,5,16,128]{4,3,2,1,0:T(8,128)S(1)} %get-tuple-element.10.halo, f32[8,16,256]{2,1,0:T(8,128)S(1)} %get-tuple-element.11.vector, f32[2,8,16,128]{3,2,1,0:T(8,128)S(1)} %get-tuple-element.12.vector_halo, ...), custom_call_target="tpu_custom_call" | custom-call | tf_op jit(solution)/shard_map/pallas_call | solution.py:954
  39.2 0.0 copy-done.1
  39.2 0.0 copy-done.3
  39.2 14.8 %shard_map.61 = (f32[8,16,256]{2,1,0:T(8,128)S(1)}, f32[2,8]{1,0:T(2,128)S(1)}) custom-call(f32[8,16,256]{2,1,0:T(8,128)S(1)} %copy-done.1, f32[8,16,256]{2,1,0:T(8,128)S(1)} %copy-done.3, f32[8,16,256]{2,1,0:T(8,128)S(1)} %get-tuple-element.14.solved, f32[1,128]{1,0:T(1,128)S(1)} %get-tuple-element.15.told), custom_call_target="tpu_custom_call" | custom-call | tf_op jit(solution)/shard_map/pallas_call | solution.py:962
  54.0 0.7 %copy.8 = f32[8,16,256]{2,1,0:T(8,128)} copy(f32[8,16,256]{2,1,0:T(8,128)S(1)} %get-tuple-element.18) | data formatting | bytes 262144
  54.7 0.6 %copy.9 = f32[2,8]{1,0:T(2,128)} copy(f32[2,8]{1,0:T(2,128)S(1)} %get-tuple-element.19) | data formatting | bytes 128
Async XLA Ops:
  0.6 0.9 %copy-start = (f32[8,16,256]{2,1,0:T(8,128)S(1)}, f32[8,16,256]{2,1,0:T(8,128)}, u32[]{:S(2)}) copy-start(f32[8,16,256]{2,1,0:T(8,128)} %vector_in.3) | copy-start | bytes 393220
  1.5 0.9 %copy-start.2 = (f32[8,16,256]{2,1,0:T(8,128)S(1)}, f32[8,16,256]{2,1,0:T(8,128)}, u32[]{:S(2)}) copy-start(f32[8,16,256]{2,1,0:T(8,128)} %previous_in.3) | copy-start | bytes 393220
  2.4 0.8 %copy-start.4 = (f32[4,16,256]{2,1,0:T(8,128)S(1)}, f32[4,16,256]{2,1,0:T(8,128)}, u32[]{:S(2)}) copy-start(f32[4,16,256]{2,1,0:T(8,128)} %conductance.1) | copy-start | bytes 196612
  3.3 0.7 %copy-start.5 = (f32[16,256]{1,0:T(8,128)S(1)}, f32[16,256]{1,0:T(8,128)}, u32[]{:S(2)}) copy-start(f32[16,256]{1,0:T(8,128)} %shift.1) | copy-start | bytes 49156
  27.0 12.2 %copy-start.1 = (f32[8,16,256]{2,1,0:T(8,128)S(1)}, f32[8,16,256]{2,1,0:T(8,128)}, u32[]{:S(2)}) copy-start(f32[8,16,256]{2,1,0:T(8,128)} %vector_in.3) | copy-start | bytes 393220
  27.0 12.1 %copy-start.3 = (f32[8,16,256]{2,1,0:T(8,128)S(1)}, f32[8,16,256]{2,1,0:T(8,128)}, u32[]{:S(2)}) copy-start(f32[8,16,256]{2,1,0:T(8,128)} %previous_in.3) | copy-start | bytes 393220
where the time goes:
time: 55.4 us; the launch traced here: 55.2 us
  Pallas kernels  49.9 us (90%)
  local copies, waits for them, and re-layouts  4.59 us (8%)
  between operations  0.67 us (1%)
    pallas_call x1, Pallas kernels, local(): pl.pallas_call(gather_kernel, out_shape=(shape(8, 5, ROWS, COLS), shape(8...  23 us
    pallas_call x1, Pallas kernels, local(): pl.pallas_call(finish_kernel, out_shape=(shape(8, ROWS, COLS), shape(2, 8...  14.8 us
    pallas_call x1, Pallas kernels, local(): pl.pallas_call(compute_kernel, out_shape=(shape(8, ROWS, COLS), shape(1,...  12.1 us
    unnamed x14, local copies, waits for them, and re-layouts  4.59 us

commit v1 on v0

--- a/solution.py
+++ b/solution.py
@@ -10,6 +10,7 @@
 EPSILON = 1e-06
 LANES = 128
 SUB = 8
+WHOLE = 99
 ROWS = 16
 COLS = 256
 MESH = pl.DeviceIdType.MESH
@@ -56,13 +57,21 @@
         return (self.rows, self.phases, SUB, LANES)
 
     def put(self, ref, t, r, x):
-        ref[t + 1, r + 1] = x
+        places = [(r + 1, x)]
         if r == 0:
-            ref[t + 1, self.phases + 1] = turn_lanes(x, -self.stride)
+            places.append((self.phases + 1, turn_lanes(x, -self.stride)))
         if r == self.phases - 1:
-            ref[t + 1, 0] = turn_lanes(x, self.stride)
-
-    def wrap(self, ref, colour=None):
+            places.append((0, turn_lanes(x, self.stride)))
+        for place, y in places:
+            ref[t + 1, place] = y
+            if isinstance(t, int) and t == 0:
+                ref[self.rows + 1, place] = turn_strips(y, -1)
+            if isinstance(t, int) and t == self.rows - 1:
+                ref[0, place] = turn_strips(y, 1)
+
+    def wrap(self, ref, per, colour=None):
+        if per >= self.rows:
+            return
         for r in range(-1, self.phases + 1):
             if colour is None or (self.rows - 1 + r) % 2 == colour:
                 ref[0, r + 1] = turn_strips(ref[self.rows, r + 1], 1)
@@ -172,7 +181,7 @@
                         grid.put(out, t, r, x)
 
         self.pairs(body)
-        grid.wrap(out, colour)
+        grid.wrap(out, self.per, colour)
         self.now[colour] = out
 
     def smooth_from_zero(self):
@@ -202,7 +211,7 @@
                     grid.put(self.residual, t, r, self.dia[t, r] * x)
 
         self.pairs(body)
-        grid.wrap(self.residual)
+        grid.wrap(self.residual, self.per)
 
     def find_weights(self):
         grid, dense, edge = self.grid, DENSE[self.index], self.edge
@@ -224,7 +233,7 @@
 
         rows(dense.rows, edges, self.per)
         for index in range(4):
-            dense.wrap(self.weights.at[index])
+            dense.wrap(self.weights.at[index], self.per)
         w = self.weight
 
         def corners(i):
@@ -239,7 +248,7 @@
 
         rows(dense.rows, corners, self.per)
         for index in range(4, 8):
-            dense.wrap(self.weights.at[index])
+            dense.wrap(self.weights.at[index], self.per)
 
     def weight(self, index, i, p):
         return self.weights[index, i + 1, p + 1]
@@ -366,7 +375,7 @@
 
         rows(dense.rows, body, self.per)
         for index in range(6):
-            dense.wrap(self.passed.at[index])
+            dense.wrap(self.passed.at[index], self.per)
 
     def give_product(self, coarse):
         dense, grid = DENSE[self.index], coarse.grid
@@ -391,7 +400,7 @@
 
         rows(dense.rows, body, coarse.per)
         for index in range(4):
-            grid.wrap(coarse.own.at[index])
+            grid.wrap(coarse.own.at[index], coarse.per)
 
         def scaled(u):
             for odd in (0, 1):
@@ -429,7 +438,7 @@
                     coarse.grid.put(coarse.right, i, phase, y * coarse.inv[i, phase])
 
         rows(dense.rows, body, coarse.per)
-        coarse.grid.wrap(coarse.right)
+        coarse.grid.wrap(coarse.right, coarse.per)
 
     def prolong(self, coarse):
         grid, dense, w = self.grid, DENSE[self.index], self.weight
@@ -442,7 +451,6 @@
                 first = coarse.now[i % 2][i + 1, 1]
                 second = turn_lanes(coarse.now[(i + 1) % 2][i + 1, 2], dense.stride)
                 dense.put(self.lifted, i, 0, jnp.where(even, first, second))
-            dense.wrap(self.lifted)
             e = lambda i, p, parity: self.lifted[i + 1, p + 1]
         outs = [self.spare(0), self.spare(1)]
 
@@ -472,7 +480,7 @@
 
         rows(dense.rows // 2, body, self.per)
         for colour in (0, 1):
-            grid.wrap(outs[colour], colour)
+            grid.wrap(outs[colour], self.per, colour)
             self.now[colour] = outs[colour]
 
 
@@ -535,9 +543,9 @@
                     x = x * west_ok
                 grid.put(level.own.at[index], t, r, x)
 
-    rows(ROWS, body, 2)
+    rows(ROWS, body, level.per)
     for index in range(4):
-        grid.wrap(level.own.at[index])
+        grid.wrap(level.own.at[index], level.per)
 
     def scaled(t):
         shift = phases_of(4, t, own_out, halo_out, low)
@@ -547,7 +555,7 @@
             total = (pairs[0] + pairs[1]) + (pairs[2] + pairs[3])
             level.scale_edges(t, r, edges, shift[r] + total)
 
-    rows(ROWS, scaled, 2)
+    rows(ROWS, scaled, level.per)
 
 
 def fill_right(level, own_out, halo_out):
@@ -560,8 +568,8 @@
         for r, x in enumerate(phases_of(5, t, own_out, halo_out, low)):
             grid.put(vector, t, r, x)
 
-    rows(ROWS, body, 4)
-    grid.wrap(vector)
+    rows(ROWS, body, level.per)
+    grid.wrap(vector, level.per)
 
     def image(u):
         for odd in (0, 1):
@@ -571,7 +579,7 @@
                 grid.put(level.right, t, r, x)
 
     level.pairs(image)
-    grid.wrap(level.right)
+    grid.wrap(level.right, level.per)
 
 
 def setup(levels):
@@ -624,52 +632,71 @@
     return alpha, scale
 
 
-def compute(col_place, own, halo, vector, vector_halo, previous, solved, told, levels_refs, own_out, halo_out, phased):
-    levels = [Level(index, refs, 2 if index == 0 else 99) for index, refs in enumerate(levels_refs)]
-    own_order = phase_matrix(False, False)
-    halo_order = phase_matrix(True, False)
-    whole = (SUB * ROWS, COLS)
-    half = (SUB * ROWS, LANES)
+def spread_edges(own, halo, own_out, halo_out):
+    own_order, halo_order = phase_matrix(False, False), phase_matrix(True, False)
     for field in range(5):
-        sides = [halo[:, side, field].reshape(half) for side in (0, 1)]
+        sides = [halo[:, side, field].reshape(SUB * ROWS, LANES) for side in (0, 1)]
         spread(
             field,
-            own[:, field].reshape(whole),
+            own[:, field].reshape(SUB * ROWS, COLS),
             jnp.concatenate(sides, axis=1),
             own_order,
             halo_order,
             own_out,
             halo_out,
         )
-    sides = [vector_halo[side].reshape(half) for side in (0, 1)]
+
+
+def spread_vector(vector, vector_halo, own_out, halo_out):
+    sides = [vector_halo[side].reshape(SUB * ROWS, LANES) for side in (0, 1)]
     spread(
         5,
-        vector[...].reshape(whole),
+        vector[...].reshape(SUB * ROWS, COLS),
         jnp.concatenate(sides, axis=1),
-        own_order,
-        halo_order,
+        phase_matrix(False, False),
+        phase_matrix(True, False),
         own_out,
         halo_out,
     )
-    fill_edges(levels[0], col_place, own_out, halo_out)
-    fill_right(levels[0], own_out, halo_out)
-    setup(levels)
-    cycle(levels, 0)
+
+
+def take_solved(level, phased, solved):
     lane = lax.broadcasted_iota(jnp.int32, (SUB, LANES), 1)
     low = lane < 64
 
     def gather(u):
         for odd in (0, 1):
             t = 2 * u + odd
-            x = [levels[0].now[(odd + r) % 2][t + 1, r + 1] for r in range(4)]
+            x = [level.now[(odd + r) % 2][t + 1, r + 1] for r in range(4)]
             for pair in (0, 1):
                 y = jnp.where(low, x[2 * pair], turn_lanes(x[2 * pair + 1], 64))
                 phased.at[pair][pl.ds(t, SUB, stride=ROWS), :] = y
 
-    rows(ROWS // 2, gather, 2)
-    result = reorder(jnp.concatenate([phased[0], phased[1]], axis=1), phase_matrix(False, True))
+    rows(ROWS // 2, gather, level.per)
+    result = reorder(
+        jnp.concatenate([phased[0], phased[1]], axis=1), phase_matrix(False, True)
+    )
     solved[...] = result.reshape(SUB, ROWS, COLS)
-    told[...] = tell(result, vector[...].reshape(whole), previous[...].reshape(whole))
+
+
+def compute(
+    col_place, own, halo, vector, vector_halo, previous, solved, told, levels_refs, own_out, halo_out, phased, waits
+):
+    wait_vectors, wait_previous = waits
+    levels = [Level(index, refs, WHOLE) for index, refs in enumerate(levels_refs)]
+    spread_edges(own, halo, own_out, halo_out)
+    fill_edges(levels[0], col_place, own_out, halo_out)
+    setup(levels)
+    wait_vectors()
+    spread_vector(vector, vector_halo, own_out, halo_out)
+    fill_right(levels[0], own_out, halo_out)
+    cycle(levels, 0)
+    take_solved(levels[0], phased, solved)
+    wait_previous()
+    whole = (SUB * ROWS, COLS)
+    told[...] = tell(
+        solved[...].reshape(whole), vector[...].reshape(whole), previous[...].reshape(whole)
+    )
 
 
 def copy_out(source, target, send, receive, grp, col):
@@ -819,16 +846,22 @@
                     )
                 )
             )
-    for copy in from_twin + halves + side_vectors:
+    for copy in from_twin + halves:
         copy.wait_recv()
 
-    def finish():
+    def wait_vectors():
+        for copy in side_vectors:
+            copy.wait_recv()
+
+    def wait_previous():
         for copy in previouses:
             copy.wait_recv()
+
+    def wait_sends():
         for copy in started:
             copy.wait_send()
 
-    return finish
+    return wait_vectors, wait_previous, wait_sends
 
 
 def finish_semaphores():
@@ -897,6 +930,7 @@
 
 
 VMEM = pl.BlockSpec(memory_space=pltpu.VMEM)
+ANY = pl.BlockSpec(memory_space=pl.ANY)
 LIMIT = 48 * 1024 * 1024
 
 
@@ -904,69 +938,74 @@
     return jax.ShapeDtypeStruct(dims, F32)
 
 
-def gather_kernel(conductance, shift, vector_in, previous_in, own, halo, vector, vector_halo, previous, *semaphores):
-    g, c = lax.axis_index("grp"), lax.axis_index("col")
-    n_col = lax.axis_size("col")
-    gather_sources(g, conductance, shift, vector_in, previous_in, own, vector, previous)
-    greet(
-        [((g + step) % 8, c) for step in range(1, 8)]
-        + [(g, (c + 1) % n_col), (g, (c + n_col - 1) % n_col)]
-    )
-    gather(g, c, vector_in, previous_in, own, halo, vector, vector_halo, previous, semaphores)()
-
-
-def compute_kernel(own, halo, vector, vector_halo, previous, solved, told, *scratch):
+def step_kernel(conductance, shift, vector_hbm, previous_hbm, out, coefficients, *scratch):
     leaves, tree = flat_levels()
     count = len(leaves)
     levels_refs = jax.tree.unflatten(tree, scratch[:count])
-    own_out, halo_out, phased = scratch[count:]
-    c = lax.axis_index("col")
-    compute(c, own, halo, vector, vector_halo, previous, solved, told, levels_refs, own_out, halo_out, phased)
-
-
-def finish_kernel(vector_in, previous_in, solved, told, out, coefficients, got, heard, verdicts, *semaphores):
+    (own_out, halo_out, phased, vector_in, previous_in, own, halo, vector, vector_halo, previous, solved, told, got, heard, verdicts, loads) = scratch[count : count + 16]
+    semaphores = scratch[count + 16 :]
     g, c = lax.axis_index("grp"), lax.axis_index("col")
     n_col = lax.axis_size("col")
-    greet(
-        [((g + step) % 8, c) for step in range(1, 8)]
-        + [(g, (c + step) % n_col) for step in range(1, n_col)]
+    loading = [
+        pltpu.make_async_copy(conductance, own.at[g, pl.ds(0, 4)], loads.at[0]),
+        pltpu.make_async_copy(shift, own.at[g, 4], loads.at[1]),
+        pltpu.make_async_copy(vector_hbm, vector_in, loads.at[2]),
+        pltpu.make_async_copy(previous_hbm, previous_in, loads.at[3]),
+    ]
+    for copy in loading:
+        copy.start()
+    barrier = pltpu.get_barrier_semaphore()
+    partners = [((g + step) % 8, c) for step in range(1, 8)]
+    partners += [(g, (c + step) % n_col) for step in range(1, n_col)]
+    for grp, col in partners:
+        pl.semaphore_signal(barrier, inc=1, device_id=(grp, col), device_id_type=MESH)
+    for copy in loading:
+        copy.wait()
+    vector[g] = vector_in[g]
+    previous[g] = previous_in[g]
+    pl.semaphore_wait(barrier, len(partners))
+    wait_vectors, wait_previous, wait_sends = gather(
+        g, c, vector_in, previous_in, own, halo, vector, vector_halo, previous, semaphores[:7]
     )
-    conclude_all(g, c, vector_in, previous_in, solved, told, got, heard, verdicts, out, coefficients, semaphores)
+    compute(c, own, halo, vector, vector_halo, previous, solved, told, levels_refs, own_out, halo_out, phased, (wait_vectors, wait_previous))
+    conclude_all(g, c, vector_in, previous_in, solved, told, got, heard, verdicts, out, coefficients, semaphores[7:])
+    wait_sends()
 
 
 def local(conductance, shift, vector_in, previous_in):
     n_col = lax.axis_size("col")
-    gathered = pl.pallas_call(
-        gather_kernel,
-        out_shape=(
-            shape(8, 5, ROWS, COLS),
-            shape(8, 2, 5, ROWS, LANES),
-            shape(8, ROWS, COLS),
-            shape(2, 8, ROWS, LANES),
-            shape(8, ROWS, COLS),
+    leaves, _ = flat_levels()
+    tile = (8, ROWS, COLS)
+    return pl.pallas_call(
+        step_kernel,
+        out_shape=(shape(8, ROWS, COLS), shape(2, 8)),
+        in_specs=[ANY] * 4,
+        out_specs=(VMEM,) * 2,
+        scratch_shapes=leaves
+        + spread_scratch()
+        + [
+            pltpu.VMEM(dims, F32)
+            for dims in (
+                tile,
+                tile,
+                (8, 5, ROWS, COLS),
+                (8, 2, 5, ROWS, LANES),
+                tile,
+                (2, 8, ROWS, LANES),
+                tile,
+                tile,
+                (1, LANES),
+            )
+        ]
+        + finish_scratch(n_col)
+        + [pltpu.SemaphoreType.DMA((4,))]
+        + gather_semaphores()
+        + finish_semaphores(),
+        compiler_params=pltpu.CompilerParams(
+            collective_id=0, has_side_effects=True, vmem_limit_bytes=LIMIT
         ),
-        in_specs=[VMEM] * 4,
-        out_specs=(VMEM,) * 5,
-        scratch_shapes=gather_semaphores(),
-        compiler_params=pltpu.CompilerParams(collective_id=0, has_side_effects=True, vmem_limit_bytes=LIMIT),
+        name="lanczos_step",
     )(conductance, shift, vector_in, previous_in)
-    leaves, _ = flat_levels()
-    solved, told = pl.pallas_call(
-        compute_kernel,
-        out_shape=(shape(8, ROWS, COLS), shape(1, LANES)),
-        in_specs=[VMEM] * 5,
-        out_specs=(VMEM,) * 2,
-        scratch_shapes=leaves + spread_scratch(),
-        compiler_params=pltpu.CompilerParams(vmem_limit_bytes=LIMIT),
-    )(*gathered)
-    return pl.pallas_call(
-        finish_kernel,
-        out_shape=(shape(8, ROWS, COLS), shape(2, 8)),
-        in_specs=[VMEM] * 4,
-        out_specs=(VMEM,) * 2,
-        scratch_shapes=finish_scratch(n_col) + finish_semaphores(),
-        compiler_params=pltpu.CompilerParams(collective_id=1, has_side_effects=True, vmem_limit_bytes=LIMIT),
-    )(vector_in, previous_in, solved, told)
 
 
 def solution(mesh):

time: 55.4 us -> 44.5 us (0.80)
  Pallas kernels: 49.9 us -> 39.1 us
    pallas_call x3 -> x1, Pallas kernels: 49.9 us -> 39.1 us  [local(): pl.pallas_call(step_kernel, out_shape=(shape(8, ROWS, COLS), shape(2, 8))...]
    unnamed x14 -> x10, local copies, waits for them, and re-layouts: 4.59 us -> 4.58 us
where the time goes in v1:
time: 44.5 us; the launch traced here: 44.3 us
  Pallas kernels  39.1 us (88%)
  local copies, waits for them, and re-layouts  4.58 us (10%)
  between operations  0.65 us (1%)
    pallas_call x1, Pallas kernels, local(): pl.pallas_call(step_kernel, out_shape=(shape(8, ROWS, COLS), shape(2, 8))...  39.1 us
    unnamed x10, local copies, waits for them, and re-layouts  4.58 us

profile of v1, /device:TPU:1, one launch (start us, length us, event | category | flops | bytes accessed | tf_op | source)
XLA Modules:
  0.0 44.3 jit_solution(14879960375947123203)
XLA Ops:
  0.6 0.0 copy-start
  0.6 0.9 %copy-done = f32[8,16,256]{2,1,0:T(8,128)S(1)} copy-done((f32[8,16,256]{2,1,0:T(8,128)S(1)}, f32[8,16,256]{2,1,0:T(8,128)}, u32[]{:S(2)}) %copy-start) | copy-done | bytes 131096
  1.5 0.0 copy-start.1
  1.5 0.9 %copy-done.1 = f32[8,16,256]{2,1,0:T(8,128)S(1)} copy-done((f32[8,16,256]{2,1,0:T(8,128)S(1)}, f32[8,16,256]{2,1,0:T(8,128)}, u32[]{:S(2)}) %copy-start.1) | copy-done | bytes 131096
  2.4 0.0 copy-start.2
  2.4 0.8 %copy-done.2 = f32[4,16,256]{2,1,0:T(8,128)S(1)} copy-done((f32[4,16,256]{2,1,0:T(8,128)S(1)}, f32[4,16,256]{2,1,0:T(8,128)}, u32[]{:S(2)}) %copy-start.2) | copy-done | bytes 65560
  3.3 0.0 copy-start.3
  3.3 0.7 %copy-done.3 = f32[16,256]{1,0:T(8,128)S(1)} copy-done((f32[16,256]{1,0:T(8,128)S(1)}, f32[16,256]{1,0:T(8,128)}, u32[]{:S(2)}) %copy-start.3) | copy-done | bytes 16408
  4.0 39.1 %lanczos_step.1 = (f32[8,16,256]{2,1,0:T(8,128)S(1)}, f32[2,8]{1,0:T(2,128)S(1)}) custom-call(f32[4,16,256]{2,1,0:T(8,128)S(1)} %copy-done.2, f32[16,256]{1,0:T(8,128)S(1)} %copy-done.3, f32[8,16,256]{2,1,0:T(8,128)S(1)} %copy-done, f32[8,16,256]{2,1,0:T(8,128)S(1)} %copy-done.1), custom_call_target="tpu_custom_call" | custom-call | tf_op jit(solution)/shard_map/lanczos_step/pallas_call | solution.py:979
  43.1 0.7 %copy.8 = f32[8,16,256]{2,1,0:T(8,128)} copy(f32[8,16,256]{2,1,0:T(8,128)S(1)} %get-tuple-element.4) | data formatting | bytes 262144
  43.7 0.6 %copy.9 = f32[2,8]{1,0:T(2,128)} copy(f32[2,8]{1,0:T(2,128)S(1)} %get-tuple-element.5) | data formatting | bytes 128
Async XLA Ops:
  0.6 0.9 %copy-start = (f32[8,16,256]{2,1,0:T(8,128)S(1)}, f32[8,16,256]{2,1,0:T(8,128)}, u32[]{:S(2)}) copy-start(f32[8,16,256]{2,1,0:T(8,128)} %vector_hbm.1) | copy-start | bytes 393220
  1.5 0.9 %copy-start.1 = (f32[8,16,256]{2,1,0:T(8,128)S(1)}, f32[8,16,256]{2,1,0:T(8,128)}, u32[]{:S(2)}) copy-start(f32[8,16,256]{2,1,0:T(8,128)} %previous_hbm.1) | copy-start | bytes 393220
  2.4 0.8 %copy-start.2 = (f32[4,16,256]{2,1,0:T(8,128)S(1)}, f32[4,16,256]{2,1,0:T(8,128)}, u32[]{:S(2)}) copy-start(f32[4,16,256]{2,1,0:T(8,128)} %conductance.1) | copy-start | bytes 196612
  3.3 0.7 %copy-start.3 = (f32[16,256]{1,0:T(8,128)S(1)}, f32[16,256]{1,0:T(8,128)}, u32[]{:S(2)}) copy-start(f32[16,256]{1,0:T(8,128)} %shift.1) | copy-start | bytes 49156

commit v2 on v1

--- a/solution.py
+++ b/solution.py
@@ -503,10 +503,10 @@
     return jnp.where(phased == target, 1.0, 0.0).astype(BF16)
 
 
-def spread(field, own, halo, own_order, halo_order, own_out, halo_out):
-    for out, x in ((own_out, reorder(own, own_order)), (halo_out, reorder(halo, halo_order))):
-        for pair in (0, 1):
-            out[field, pair] = x[:, pair * LANES : (pair + 1) * LANES]
+def reordered(x, order, out):
+    moved = reorder(x, order)
+    for pair in (0, 1):
+        out[pair] = moved[:, pair * LANES : (pair + 1) * LANES]
 
 
 def phases_of(field, t, own_out, halo_out, low):
@@ -632,71 +632,55 @@
     return alpha, scale
 
 
-def spread_edges(own, halo, own_out, halo_out):
-    own_order, halo_order = phase_matrix(False, False), phase_matrix(True, False)
+def spread_own(own, own_out):
+    order = phase_matrix(False, False)
+    for field in range(5):
+        reordered(own[:, field].reshape(SUB * ROWS, COLS), order, own_out.at[field])
+
+
+def spread_halo(halo, halo_out):
+    order = phase_matrix(True, False)
     for field in range(5):
         sides = [halo[:, side, field].reshape(SUB * ROWS, LANES) for side in (0, 1)]
-        spread(
-            field,
-            own[:, field].reshape(SUB * ROWS, COLS),
-            jnp.concatenate(sides, axis=1),
-            own_order,
-            halo_order,
-            own_out,
-            halo_out,
-        )
+        reordered(jnp.concatenate(sides, axis=1), order, halo_out.at[field])
 
 
 def spread_vector(vector, vector_halo, own_out, halo_out):
+    reordered(vector[...].reshape(SUB * ROWS, COLS), phase_matrix(False, False), own_out.at[5])
     sides = [vector_halo[side].reshape(SUB * ROWS, LANES) for side in (0, 1)]
-    spread(
-        5,
-        vector[...].reshape(SUB * ROWS, COLS),
-        jnp.concatenate(sides, axis=1),
-        phase_matrix(False, False),
-        phase_matrix(True, False),
-        own_out,
-        halo_out,
-    )
-
-
-def take_solved(level, phased, solved):
+    reordered(jnp.concatenate(sides, axis=1), phase_matrix(True, False), halo_out.at[5])
+
+
+def pack_solved(level, phased):
     lane = lax.broadcasted_iota(jnp.int32, (SUB, LANES), 1)
     low = lane < 64
-
-    def gather(u):
-        for odd in (0, 1):
-            t = 2 * u + odd
-            x = [level.now[(odd + r) % 2][t + 1, r + 1] for r in range(4)]
-            for pair in (0, 1):
-                y = jnp.where(low, x[2 * pair], turn_lanes(x[2 * pair + 1], 64))
-                phased.at[pair][pl.ds(t, SUB, stride=ROWS), :] = y
-
-    rows(ROWS // 2, gather, level.per)
-    result = reorder(
-        jnp.concatenate([phased[0], phased[1]], axis=1), phase_matrix(False, True)
-    )
-    solved[...] = result.reshape(SUB, ROWS, COLS)
+    for t in range(ROWS):
+        x = [level.now[(t + r) % 2][t + 1, r + 1] for r in range(4)]
+        for pair in (0, 1):
+            y = jnp.where(low, x[2 * pair], turn_lanes(x[2 * pair + 1], 64))
+            phased.at[pair][pl.ds(t, SUB, stride=ROWS), :] = y
 
 
 def compute(
-    col_place, own, halo, vector, vector_halo, previous, solved, told, levels_refs, own_out, halo_out, phased, waits
+    col_place, halo, vector, vector_halo, previous, levels_refs, own_out, halo_out, phased, before, waits
 ):
     wait_vectors, wait_previous = waits
     levels = [Level(index, refs, WHOLE) for index, refs in enumerate(levels_refs)]
-    spread_edges(own, halo, own_out, halo_out)
+    spread_halo(halo, halo_out)
     fill_edges(levels[0], col_place, own_out, halo_out)
     setup(levels)
     wait_vectors()
     spread_vector(vector, vector_halo, own_out, halo_out)
     fill_right(levels[0], own_out, halo_out)
+    wait_previous()
+    reordered(previous[...].reshape(SUB * ROWS, COLS), phase_matrix(False, False), before)
     cycle(levels, 0)
-    take_solved(levels[0], phased, solved)
-    wait_previous()
-    whole = (SUB * ROWS, COLS)
-    told[...] = tell(
-        solved[...].reshape(whole), vector[...].reshape(whole), previous[...].reshape(whole)
-    )
+    pack_solved(levels[0], phased)
+
+
+def make_told(told, phased, own_out, before):
+    flat = (2 * SUB * ROWS, LANES)
+    told[...] = tell(phased[...].reshape(flat), own_out[5].reshape(flat), before[...].reshape(flat))
 
 
 def copy_out(source, target, send, receive, grp, col):
@@ -719,7 +703,11 @@
 
 def gather_semaphores():
     dma = pltpu.SemaphoreType.DMA
-    return [dma((2, 3)), dma((2, 7)), dma((2, 7)), dma((2, 8)), dma((2, 2)), dma((2, 4)), dma((2, 8))]
+    return [dma((4,)), dma((2,)), dma((2,)), dma((5,)), dma((2,)), dma((2,)), dma((2,))]
+
+
+def wait_bytes(ref, semaphore):
+    pltpu.make_async_copy(ref, ref, semaphore).wait()
 
 
 def gather_sources(g, conductance, shift, vector_in, previous_in, own, vector, previous):
@@ -729,196 +717,149 @@
     previous[g] = previous_in[g]
 
 
-def gather(g, c, vector_in, previous_in, own, halo, vector, vector_halo, previous, semaphores):
+def gather(g, c, vector_in, previous_in, own, halo, vector, vector_halo, previous, semaphores, while_waiting):
     along, of_vector, of_previous, beside, vector_beside, across, halo_across = semaphores
     n_grp, n_col = 8, lax.axis_size("col")
     y, core = g // 2, g % 2
     twin = y * 2 + 1 - core
     mates = [(g + step) % n_grp for step in range(1, n_grp)]
     east, west = (c + 1) % n_col, (c + n_col - 1) % n_col
-    started = []
-
-    def start(copy):
-        copy.start()
-        started.append(copy)
-        return copy
 
     def place(back):
         return ((y + 4 - back) % 4) * 2 + core
 
     def send_sides(back):
-        rows_ = place(back)
-        return [
-            start(
-                copy_out(
-                    own.at[rows_, :, :, pl.ds(LANES, LANES)],
-                    halo.at[rows_, 1],
-                    beside.at[0, back],
-                    beside.at[1, back],
-                    g,
-                    east,
-                )
-            ),
-            start(
-                copy_out(
-                    own.at[rows_, :, :, pl.ds(0, LANES)],
-                    halo.at[rows_, 0],
-                    beside.at[0, 4 + back],
-                    beside.at[1, 4 + back],
-                    g,
-                    west,
-                )
-            ),
-        ]
-
-    def send_across(back):
-        rows_ = place(back)
-        return start(
-            copy_out(own.at[rows_], own.at[rows_], across.at[0, back], across.at[1, back], twin, c)
-        )
-
-    arriving = []
-    for step in range(1, 4):
+        row = place(back)
+        for side, to in ((1, east), (0, west)):
+            copy_out(
+                own.at[row, :, :, pl.ds(side * LANES, LANES)],
+                halo.at[row, side],
+                beside.at[4],
+                beside.at[back],
+                g,
+                to,
+            ).start()
+
+    def pass_tile(back):
+        row = place(back)
+        copy_out(own.at[row], own.at[row], across.at[0], across.at[1], twin, c).start()
+
+    def pass_sides(back):
+        row = place(back)
+        wait_bytes(halo.at[row], beside.at[back])
+        copy_out(halo.at[row], halo.at[row], halo_across.at[0], halo_across.at[1], twin, c).start()
+
+    def transpose(source, target, semaphore):
+        for to in mates:
+            copy_out(source.at[to], target.at[g], semaphore.at[0], semaphore.at[1], to, c).start()
+
+    for step in (1, 3, 2):
         to = ((y + step) % 4) * 2 + core
-        arriving.append(
-            start(
-                copy_out(own.at[g], own.at[g], along.at[0, step - 1], along.at[1, step - 1], to, c)
-            )
-        )
-    from_sides = [send_sides(0)]
-    from_twin = [send_across(0)]
-    vectors = [
-        start(
-            copy_out(
-                vector_in.at[to], vector.at[g], of_vector.at[0, i], of_vector.at[1, i], to, c
-            )
-        )
-        for i, to in enumerate(mates)
-    ]
+        copy_out(own.at[g], own.at[g], along.at[0], along.at[step], to, c).start()
+    send_sides(0)
+    pass_tile(0)
+    transpose(vector_in, vector, of_vector)
     for back in (1, 3, 2):
-        arriving[back - 1].wait_recv()
-        from_sides.append(send_sides(back))
-        from_twin.append(send_across(back))
-    for copy in vectors:
-        copy.wait_recv()
-    side_vectors = []
+        row = place(back)
+        wait_bytes(own.at[row], along.at[back])
+        send_sides(back)
+        pass_tile(back)
+    wait_bytes(vector.at[pl.ds(0, n_grp - 1)], of_vector.at[1])
     for side, to in ((1, east), (0, west)):
-        side_vectors.append(
-            start(
-                copy_out(
-                    vector.at[:, :, pl.ds(side * LANES, LANES)],
-                    vector_halo.at[side],
-                    vector_beside.at[0, side],
-                    vector_beside.at[1, side],
-                    g,
-                    to,
-                )
-            )
-        )
-    previouses = [
-        start(
-            copy_out(
-                previous_in.at[to],
-                previous.at[g],
-                of_previous.at[0, i],
-                of_previous.at[1, i],
-                to,
-                c,
-            )
-        )
-        for i, to in enumerate(mates)
-    ]
-    halves = []
-    for order, back in enumerate((0, 1, 3, 2)):
-        for side in (1, 0):
-            from_sides[order][1 - side].wait_recv()
-            rows_ = place(back)
-            at = side * 4 + back
-            halves.append(
-                start(
-                    copy_out(
-                        halo.at[rows_, side],
-                        halo.at[rows_, side],
-                        halo_across.at[0, at],
-                        halo_across.at[1, at],
-                        twin,
-                        c,
-                    )
-                )
-            )
-    for copy in from_twin + halves:
-        copy.wait_recv()
+        copy_out(
+            vector.at[:, :, pl.ds(side * LANES, LANES)],
+            vector_halo.at[side],
+            vector_beside.at[0],
+            vector_beside.at[1],
+            g,
+            to,
+        ).start()
+    transpose(previous_in, previous, of_previous)
+    for back in (0, 1, 3):
+        pass_sides(back)
+    wait_bytes(own.at[pl.ds(0, 4)], across.at[1])
+    while_waiting()
+    pass_sides(2)
+    wait_bytes(halo.at[pl.ds(0, 4)], halo_across.at[1])
 
     def wait_vectors():
-        for copy in side_vectors:
-            copy.wait_recv()
+        wait_bytes(vector_halo, vector_beside.at[1])
 
     def wait_previous():
-        for copy in previouses:
-            copy.wait_recv()
+        wait_bytes(previous.at[pl.ds(0, n_grp - 1)], of_previous.at[1])
 
     def wait_sends():
-        for copy in started:
-            copy.wait_send()
+        wait_bytes(own.at[pl.ds(0, 3)], along.at[0])
+        wait_bytes(halo.at[pl.ds(0, 4)], beside.at[4])
+        wait_bytes(own.at[pl.ds(0, 4)], across.at[0])
+        wait_bytes(halo.at[pl.ds(0, 4)], halo_across.at[0])
+        wait_bytes(vector.at[pl.ds(0, n_grp - 1)], of_vector.at[0])
+        wait_bytes(previous.at[pl.ds(0, n_grp - 1)], of_previous.at[0])
+        wait_bytes(vector_halo, vector_beside.at[0])
 
     return wait_vectors, wait_previous, wait_sends
 
 
 def finish_semaphores():
     dma = pltpu.SemaphoreType.DMA
-    return [dma((2,)), dma((2, 7)), dma((2,))]
+    return [dma((2,)), dma((2,)), dma((2,)), dma((1,))]
 
 
 def finish_scratch(n_col):
     return [
-        pltpu.VMEM((8, ROWS, COLS), F32),
+        pltpu.VMEM((8, 2, ROWS, LANES), F32),
         pltpu.VMEM((n_col, 1, LANES), F32),
         pltpu.VMEM((8, 2, LANES), F32),
+        pltpu.VMEM((8, ROWS, COLS), F32),
     ]
 
 
-def conclude_all(g, c, vector_in, previous_in, solved, told, got, heard, verdicts, out, coefficients, semaphores):
-    spread_sem, back_sem, verdict_sem = semaphores
+def conclude_all(
+    g, c, vector_in, previous_in, phased, told, got, heard, verdicts, out, made, coefficients, semaphores, make_told, wait_sends
+):
+    spread_sem, back_sem, verdict_sem, out_sem = semaphores
     n_grp, n_col = 8, lax.axis_size("col")
     mates = [(g + step) % n_grp for step in range(1, n_grp)]
+    for to in mates:
+        strip = phased.at[:, pl.ds(pl.multiple_of(to * ROWS, ROWS), ROWS), :]
+        copy_out(strip, got.at[g], back_sem.at[0], back_sem.at[1], to, c).start()
+    make_told()
     heard[c] = told[...]
-    telling = []
     for step in range(1, n_col):
         to = (c + step) % n_col
-        telling.append(copy_out(told, heard.at[c], spread_sem.at[0], spread_sem.at[1], g, to))
-        telling[-1].start()
-    back = []
-    for i, to in enumerate(mates):
-        back.append(copy_out(solved.at[to], got.at[g], back_sem.at[0, i], back_sem.at[1, i], to, c))
-        back[-1].start()
-    got[g] = solved[g]
+        copy_out(told, heard.at[c], spread_sem.at[0], spread_sem.at[1], g, to).start()
+    for pair in (0, 1):
+        got[g, pair] = phased[pair, pl.ds(pl.multiple_of(g * ROWS, ROWS), ROWS), :]
+    wait_sends()
     several = heard.at[pl.ds(0, n_col - 1)]
-    pltpu.make_async_copy(several, several, spread_sem.at[1]).wait()
+    others = verdicts.at[pl.ds(0, n_grp - 1)]
+    wait_bytes(several, spread_sem.at[1])
     alpha, scale = conclude(heard[...].reshape(n_col, LANES), float(n_grp * ROWS * n_col * COLS))
     which = lax.broadcasted_iota(jnp.int32, (2, LANES), 0)
     verdicts[g] = jnp.where(which == 0, alpha, scale)
-    deciding = []
     for to in mates:
-        deciding.append(
-            copy_out(verdicts.at[g], verdicts.at[g], verdict_sem.at[0], verdict_sem.at[1], to, c)
-        )
-        deciding[-1].start()
-    for copy in back:
-        copy.wait_recv()
-    others = verdicts.at[pl.ds(0, n_grp - 1)]
-    pltpu.make_async_copy(others, others, verdict_sem.at[1]).wait()
+        copy_out(
+            verdicts.at[g], verdicts.at[g], verdict_sem.at[0], verdict_sem.at[1], to, c
+        ).start()
+    wait_bytes(got.at[pl.ds(0, n_grp - 1)], back_sem.at[1])
+    wait_bytes(got.at[pl.ds(0, n_grp - 1)], back_sem.at[0])
+    wait_bytes(several, spread_sem.at[0])
+    packed = [got[:, pair].reshape(n_grp * ROWS, LANES) for pair in (0, 1)]
+    solved = reorder(jnp.concatenate(packed, axis=1), phase_matrix(False, True))
+    target = solved.reshape(n_grp, ROWS, COLS) - previous_in[...]
+    wait_bytes(others, verdict_sem.at[1])
     lane = lax.broadcasted_iota(jnp.int32, (2, LANES), 1)
     summary = jnp.zeros((2, LANES), F32)
     for probe in range(n_grp):
         pair = verdicts[probe]
         summary = jnp.where(lane == probe, pair, summary)
-        rest = got[probe] - pair[0:1, 0:1] * vector_in[probe] - previous_in[probe]
-        out[probe] = rest * (1.0 / pair[1:2, 0:1])
+        rest = target[probe] - pair[0:1, 0:1] * vector_in[probe]
+        made[probe] = rest * (1.0 / pair[1:2, 0:1])
+    writing = pltpu.make_async_copy(made, out, out_sem.at[0])
+    writing.start()
     coefficients[...] = summary[:, 0:n_grp]
-    pltpu.make_async_copy(several, several, spread_sem.at[0]).wait()
-    pltpu.make_async_copy(others, others, verdict_sem.at[0]).wait()
-    for copy in back:
-        copy.wait_send()
+    wait_bytes(others, verdict_sem.at[0])
+    writing.wait()
 
 
 def flat_levels():
@@ -926,12 +867,12 @@
 
 
 def spread_scratch():
-    return [pltpu.VMEM((6, 2, 8 * ROWS, LANES), F32)] * 2 + [pltpu.VMEM((2, 8 * ROWS, LANES), F32)]
+    return [pltpu.VMEM((6, 2, 8 * ROWS, LANES), F32)] * 2 + [pltpu.VMEM((2, 8 * ROWS, LANES), F32)] * 2
 
 
 VMEM = pl.BlockSpec(memory_space=pltpu.VMEM)
-ANY = pl.BlockSpec(memory_space=pl.ANY)
-LIMIT = 48 * 1024 * 1024
+HBM = pl.BlockSpec(memory_space=pltpu.HBM)
+LIMIT = 127 * 1024 * 512
 
 
 def shape(*dims):
@@ -942,8 +883,8 @@
     leaves, tree = flat_levels()
     count = len(leaves)
     levels_refs = jax.tree.unflatten(tree, scratch[:count])
-    (own_out, halo_out, phased, vector_in, previous_in, own, halo, vector, vector_halo, previous, solved, told, got, heard, verdicts, loads) = scratch[count : count + 16]
-    semaphores = scratch[count + 16 :]
+    (own_out, halo_out, phased, before, vector_in, previous_in, own, halo, vector, vector_halo, previous, told, got, heard, verdicts, made, loads) = scratch[count : count + 17]
+    semaphores = scratch[count + 17 :]
     g, c = lax.axis_index("grp"), lax.axis_index("col")
     n_col = lax.axis_size("col")
     loading = [
@@ -965,11 +906,10 @@
     previous[g] = previous_in[g]
     pl.semaphore_wait(barrier, len(partners))
     wait_vectors, wait_previous, wait_sends = gather(
-        g, c, vector_in, previous_in, own, halo, vector, vector_halo, previous, semaphores[:7]
+        g, c, vector_in, previous_in, own, halo, vector, vector_halo, previous, semaphores[:7], lambda: spread_own(own, own_out)
     )
-    compute(c, own, halo, vector, vector_halo, previous, solved, told, levels_refs, own_out, halo_out, phased, (wait_vectors, wait_previous))
-    conclude_all(g, c, vector_in, previous_in, solved, told, got, heard, verdicts, out, coefficients, semaphores[7:])
-    wait_sends()
+    compute(c, halo, vector, vector_halo, previous, levels_refs, own_out, halo_out, phased, before, (wait_vectors, wait_previous))
+    conclude_all(g, c, vector_in, previous_in, phased, told, got, heard, verdicts, out, made, coefficients, semaphores[7:], lambda: make_told(told, phased, own_out, before), wait_sends)
 
 
 def local(conductance, shift, vector_in, previous_in):
@@ -979,8 +919,8 @@
     return pl.pallas_call(
         step_kernel,
         out_shape=(shape(8, ROWS, COLS), shape(2, 8)),
-        in_specs=[ANY] * 4,
-        out_specs=(VMEM,) * 2,
+        in_specs=[HBM] * 4,
+        out_specs=(HBM, VMEM),
         scratch_shapes=leaves
         + spread_scratch()
         + [
@@ -992,7 +932,6 @@
                 (8, 2, 5, ROWS, LANES),
                 tile,
                 (2, 8, ROWS, LANES),
-                tile,
                 tile,
                 (1, LANES),
             )

time: 44.5 us -> 41.3 us (0.928)
  local copies, waits for them, and re-layouts: 4.58 us -> 2.13 us
  Pallas kernels: 39.1 us -> 38.4 us
    unnamed x10 -> x4, local copies, waits for them, and re-layouts: 4.58 us -> 2.13 us
    pallas_call x1, Pallas kernels: 39.1 us -> 38.4 us  [local(): pl.pallas_call(step_kernel, out_shape=(shape(8, ROWS, COLS), shape(2, 8))...]
where the time goes in v2:
time: 41.3 us; the launch traced here: 41.2 us
  Pallas kernels  38.4 us (93%)
  local copies, waits for them, and re-layouts  2.13 us (5%)
  between operations  0.65 us (2%)
    pallas_call x1, Pallas kernels, local(): pl.pallas_call(step_kernel, out_shape=(shape(8, ROWS, COLS), shape(2, 8))...  38.4 us
    unnamed x4, local copies, waits for them, and re-layouts  2.13 us

profile of v2, /device:TPU:1, one launch (start us, length us, event | category | flops | bytes accessed | tf_op | source)
XLA Modules:
  0.0 41.2 jit_solution(17709174832333739650)
XLA Ops:
  0.6 38.4 %lanczos_step.1 = (f32[8,16,256]{2,1,0:T(8,128)}, f32[2,8]{1,0:T(2,128)}) custom-call(f32[4,16,256]{2,1,0:T(8,128)} %conductance.1, f32[16,256]{1,0:T(8,128)} %shift.1, f32[8,16,256]{2,1,0:T(8,128)} %vector_hbm.1, f32[8,16,256]{2,1,0:T(8,128)} %previous_hbm.1), custom_call_target="tpu_custom_call" | custom-call | tf_op jit(solution)/shard_map/lanczos_step/pallas_call | solution.py:919
  39.0 0.0 copy-start
  39.1 1.6 %copy.8 = f32[8,16,256]{2,1,0:T(8,128)} copy(f32[8,16,256]{2,1,0:T(8,128)} %get-tuple-element.4) | data formatting | bytes 262144
  40.6 0.0 copy-done
  40.6 0.6 %copy.9 = f32[2,8]{1,0:T(2,128)} copy(f32[2,8]{1,0:T(2,128)S(1)} %copy-done) | data formatting | bytes 128
Async XLA Ops:
  39.0 1.6 %copy-start = (f32[2,8]{1,0:T(2,128)S(1)}, f32[2,8]{1,0:T(2,128)}, u32[]{:S(2)}) copy-start(f32[2,8]{1,0:T(2,128)} %get-tuple-element.5) | copy-start | bytes 196

commit v3 on v2

--- a/solution.py
+++ b/solution.py
@@ -802,7 +802,7 @@
 
 def finish_semaphores():
     dma = pltpu.SemaphoreType.DMA
-    return [dma((2,)), dma((2,)), dma((2,)), dma((1,))]
+    return [dma((2,)), dma((2,)), dma((2,))]
 
 
 def finish_scratch(n_col):
@@ -810,14 +810,13 @@
         pltpu.VMEM((8, 2, ROWS, LANES), F32),
         pltpu.VMEM((n_col, 1, LANES), F32),
         pltpu.VMEM((8, 2, LANES), F32),
-        pltpu.VMEM((8, ROWS, COLS), F32),
     ]
 
 
 def conclude_all(
-    g, c, vector_in, previous_in, phased, told, got, heard, verdicts, out, made, coefficients, semaphores, make_told, wait_sends
+    g, c, vector_in, previous_in, phased, told, got, heard, verdicts, out, coefficients, semaphores, make_told, wait_sends
 ):
-    spread_sem, back_sem, verdict_sem, out_sem = semaphores
+    spread_sem, back_sem, verdict_sem = semaphores
     n_grp, n_col = 8, lax.axis_size("col")
     mates = [(g + step) % n_grp for step in range(1, n_grp)]
     for to in mates:
@@ -854,12 +853,11 @@
         pair = verdicts[probe]
         summary = jnp.where(lane == probe, pair, summary)
         rest = target[probe] - pair[0:1, 0:1] * vector_in[probe]
-        made[probe] = rest * (1.0 / pair[1:2, 0:1])
-    writing = pltpu.make_async_copy(made, out, out_sem.at[0])
-    writing.start()
+        made = rest * (1.0 / pair[1:2, 0:1])
+        for half in (0, 1):
+            out[2 * probe + half][...] = made[half * SUB : (half + 1) * SUB]
     coefficients[...] = summary[:, 0:n_grp]
     wait_bytes(others, verdict_sem.at[0])
-    writing.wait()
 
 
 def flat_levels():
@@ -872,19 +870,23 @@
 
 VMEM = pl.BlockSpec(memory_space=pltpu.VMEM)
 HBM = pl.BlockSpec(memory_space=pltpu.HBM)
-LIMIT = 127 * 1024 * 512
+LIMIT = 55091 * 1024
+
+
+PIECES = 16
 
 
 def shape(*dims):
     return jax.ShapeDtypeStruct(dims, F32)
 
 
-def step_kernel(conductance, shift, vector_hbm, previous_hbm, out, coefficients, *scratch):
+def step_kernel(conductance, shift, vector_hbm, previous_hbm, *rest):
+    out, coefficients, scratch = rest[:PIECES], rest[PIECES], rest[PIECES + 1 :]
     leaves, tree = flat_levels()
     count = len(leaves)
     levels_refs = jax.tree.unflatten(tree, scratch[:count])
-    (own_out, halo_out, phased, before, vector_in, previous_in, own, halo, vector, vector_halo, previous, told, got, heard, verdicts, made, loads) = scratch[count : count + 17]
-    semaphores = scratch[count + 17 :]
+    (own_out, halo_out, phased, before, vector_in, previous_in, own, halo, vector, vector_halo, previous, told, got, heard, verdicts, loads) = scratch[count : count + 16]
+    semaphores = scratch[count + 16 :]
     g, c = lax.axis_index("grp"), lax.axis_index("col")
     n_col = lax.axis_size("col")
     loading = [
@@ -909,18 +911,31 @@
         g, c, vector_in, previous_in, own, halo, vector, vector_halo, previous, semaphores[:7], lambda: spread_own(own, own_out)
     )
     compute(c, halo, vector, vector_halo, previous, levels_refs, own_out, halo_out, phased, before, (wait_vectors, wait_previous))
-    conclude_all(g, c, vector_in, previous_in, phased, told, got, heard, verdicts, out, made, coefficients, semaphores[7:], lambda: make_told(told, phased, own_out, before), wait_sends)
+    conclude_all(g, c, vector_in, previous_in, phased, told, got, heard, verdicts, out, coefficients, semaphores[7:], lambda: make_told(told, phased, own_out, before), wait_sends)
+
+
+def store_kernel(*refs):
+    made, told = refs[:PIECES], refs[PIECES]
+    out, coefficients, semaphores = refs[PIECES + 1 :]
+    copies = [pltpu.make_async_copy(told, coefficients, semaphores.at[PIECES])]
+    for piece in range(PIECES):
+        strip = out.at[piece // 2, pl.ds(piece % 2 * SUB, SUB)]
+        copies.append(pltpu.make_async_copy(made[piece], strip, semaphores.at[piece]))
+    for copy in copies:
+        copy.start()
+    for copy in copies:
+        copy.wait()
 
 
 def local(conductance, shift, vector_in, previous_in):
     n_col = lax.axis_size("col")
     leaves, _ = flat_levels()
     tile = (8, ROWS, COLS)
-    return pl.pallas_call(
+    made = pl.pallas_call(
         step_kernel,
-        out_shape=(shape(8, ROWS, COLS), shape(2, 8)),
+        out_shape=(shape(SUB, COLS),) * PIECES + (shape(2, 8),),
         in_specs=[HBM] * 4,
-        out_specs=(HBM, VMEM),
+        out_specs=(VMEM,) * (PIECES + 1),
         scratch_shapes=leaves
         + spread_scratch()
         + [
@@ -945,6 +960,15 @@
         ),
         name="lanczos_step",
     )(conductance, shift, vector_in, previous_in)
+    return pl.pallas_call(
+        store_kernel,
+        out_shape=(shape(8, ROWS, COLS), shape(2, 8)),
+        in_specs=[VMEM] * (PIECES + 1),
+        out_specs=(HBM, HBM),
+        scratch_shapes=[pltpu.SemaphoreType.DMA((PIECES + 1,))],
+        compiler_params=pltpu.CompilerParams(vmem_limit_bytes=1024 * 1024),
+        name="store",
+    )(*made)
 
 
 def solution(mesh):

time: 41.3 us -> 38.8 us (0.939)
  local copies, waits for them, and re-layouts: 2.13 us -> 0 us
    unnamed x4 -> x0, local copies, waits for them, and re-layouts: 2.13 us -> none
    pallas_call x1 -> x2, Pallas kernels: 38.4 us -> 38 us  [the longest x1 37.2 us: local(): pl.pallas_call(step_kernel, out_shape=(shape(SUB, COLS),) * PIECES + (sha...]
where the time goes in v3:
time: 38.8 us; the launch traced here: 38.7 us
  Pallas kernels  38 us (98%)
  between operations  0.64 us (2%)
    pallas_call x1, Pallas kernels, local(): pl.pallas_call(step_kernel, out_shape=(shape(SUB, COLS),) * PIECES + (sha...  37.2 us
    pallas_call x1, Pallas kernels, local(): pl.pallas_call(store_kernel, out_shape=(shape(8, ROWS, COLS), shape(2, 8)...  0.82 us

profile of v3, /device:TPU:1, one launch (start us, length us, event | category | flops | bytes accessed | tf_op | source)
XLA Modules:
  0.0 38.7 jit_solution(11226462887605405927)
XLA Ops:
  0.6 37.2 %lanczos_step.1 = (f32[8,256]{1,0:T(8,128)S(1)}, f32[8,256]{1,0:T(8,128)S(1)}, f32[8,256]{1,0:T(8,128)S(1)}, f32[8,256]{1,0:T(8,128)S(1)}, f32[8,256]{1,0:T(8,12...) custom-call(f32[4,16,256]{2,1,0:T(8,128)} %conductance.1, ...), custom_call_target="tpu_custom_call" | custom-call | tf_op jit(solution)/shard_map/lanczos_step/pallas_call | solution.py:934
  37.9 0.8 %store.1 = (f32[8,16,256]{2,1,0:T(8,128)}, f32[2,8]{1,0:T(2,128)}) custom-call(f32[8,256]{1,0:T(8,128)S(1)} %get-tuple-element.19.refs_0_, f32[8,256]{1,0:T(8,128)S(1)} %get-tuple-element.20.refs_1_, f32[8,256]{1,0:T(8,128)S(1)} %get-tuple-element.21.refs_2_, f32[8,256]{1,0:T(8,128)S(1)} %get-tuple-element.22.refs_3_, ...), custom_call_target="tpu_custom_call" | custom-call | tf_op jit(solution)/shard_map/store/pallas_call | solution.py:963

commit v4 on v3

--- a/solution.py
+++ b/solution.py
@@ -694,11 +694,16 @@
     )
 
 
-def greet(partners):
-    barrier = pltpu.get_barrier_semaphore()
-    for grp, col in partners:
-        pl.semaphore_signal(barrier, inc=1, device_id=(grp, col), device_id_type=MESH)
-    pl.semaphore_wait(barrier, len(partners))
+def group_mates(g):
+    y, core = g // 2, g % 2
+    mates = [((y + step) % 4) * 2 + k for step in (2, 1, 3) for k in (core, 1 - core)]
+    return mates + [y * 2 + 1 - core]
+
+
+def column_mates(c):
+    steps = [(dz, dx) for dz in range(8) for dx in range(4) if dz or dx]
+    steps.sort(key=lambda step: -min(step[0], 8 - step[0]) - min(step[1], 4 - step[1]))
+    return [((c // 4 + dz) % 8) * 4 + (c + dx) % 4 for dz, dx in steps]
 
 
 def gather_semaphores():
@@ -717,12 +722,12 @@
     previous[g] = previous_in[g]
 
 
-def gather(g, c, vector_in, previous_in, own, halo, vector, vector_halo, previous, semaphores, while_waiting):
+def gather(g, c, vector_in, previous_in, own, halo, vector, vector_halo, previous, semaphores, vectors_loaded, while_waiting):
     along, of_vector, of_previous, beside, vector_beside, across, halo_across = semaphores
     n_grp, n_col = 8, lax.axis_size("col")
     y, core = g // 2, g % 2
     twin = y * 2 + 1 - core
-    mates = [(g + step) % n_grp for step in range(1, n_grp)]
+    mates = group_mates(g)
     east, west = (c + 1) % n_col, (c + n_col - 1) % n_col
 
     def place(back):
@@ -758,9 +763,12 @@
         copy_out(own.at[g], own.at[g], along.at[0], along.at[step], to, c).start()
     send_sides(0)
     pass_tile(0)
+    vectors_loaded()
     transpose(vector_in, vector, of_vector)
     for back in (1, 3, 2):
         row = place(back)
+        if back == 2:
+            pass_sides(0)
         wait_bytes(own.at[row], along.at[back])
         send_sides(back)
         pass_tile(back)
@@ -775,7 +783,7 @@
             to,
         ).start()
     transpose(previous_in, previous, of_previous)
-    for back in (0, 1, 3):
+    for back in (1, 3):
         pass_sides(back)
     wait_bytes(own.at[pl.ds(0, 4)], across.at[1])
     while_waiting()
@@ -818,15 +826,14 @@
 ):
     spread_sem, back_sem, verdict_sem = semaphores
     n_grp, n_col = 8, lax.axis_size("col")
-    mates = [(g + step) % n_grp for step in range(1, n_grp)]
+    mates = group_mates(g)
+    make_told()
+    heard[c] = told[...]
+    for to in column_mates(c):
+        copy_out(told, heard.at[c], spread_sem.at[0], spread_sem.at[1], g, to).start()
     for to in mates:
         strip = phased.at[:, pl.ds(pl.multiple_of(to * ROWS, ROWS), ROWS), :]
         copy_out(strip, got.at[g], back_sem.at[0], back_sem.at[1], to, c).start()
-    make_told()
-    heard[c] = told[...]
-    for step in range(1, n_col):
-        to = (c + step) % n_col
-        copy_out(told, heard.at[c], spread_sem.at[0], spread_sem.at[1], g, to).start()
     for pair in (0, 1):
         got[g, pair] = phased[pair, pl.ds(pl.multiple_of(g * ROWS, ROWS), ROWS), :]
     wait_sends()
@@ -898,17 +905,21 @@
     for copy in loading:
         copy.start()
     barrier = pltpu.get_barrier_semaphore()
-    partners = [((g + step) % 8, c) for step in range(1, 8)]
-    partners += [(g, (c + step) % n_col) for step in range(1, n_col)]
+    partners = [(g, to) for to in column_mates(c)] + [(to, c) for to in group_mates(g)]
     for grp, col in partners:
         pl.semaphore_signal(barrier, inc=1, device_id=(grp, col), device_id_type=MESH)
-    for copy in loading:
+    for copy in loading[:2]:
         copy.wait()
-    vector[g] = vector_in[g]
-    previous[g] = previous_in[g]
+
+    def vectors_loaded():
+        for copy in loading[2:]:
+            copy.wait()
+        vector[g] = vector_in[g]
+        previous[g] = previous_in[g]
+
     pl.semaphore_wait(barrier, len(partners))
     wait_vectors, wait_previous, wait_sends = gather(
-        g, c, vector_in, previous_in, own, halo, vector, vector_halo, previous, semaphores[:7], lambda: spread_own(own, own_out)
+        g, c, vector_in, previous_in, own, halo, vector, vector_halo, previous, semaphores[:7], vectors_loaded, lambda: spread_own(own, own_out)
     )
     compute(c, halo, vector, vector_halo, previous, levels_refs, own_out, halo_out, phased, before, (wait_vectors, wait_previous))
     conclude_all(g, c, vector_in, previous_in, phased, told, got, heard, verdicts, out, coefficients, semaphores[7:], lambda: make_told(told, phased, own_out, before), wait_sends)

time: 38.8 us -> 39.1 us (level)
  no operation moved by 1% of the time
where the time goes in v4:
time: 39.1 us; the launch traced here: 39 us
  Pallas kernels  38.3 us (98%)
  between operations  0.64 us (2%)
    pallas_call x1, Pallas kernels, local(): pl.pallas_call(step_kernel, out_shape=(shape(SUB, COLS),) * PIECES + (sha...  37.5 us
    pallas_call x1, Pallas kernels, local(): pl.pallas_call(store_kernel, out_shape=(shape(8, ROWS, COLS), shape(2, 8)...  0.82 us

profile of v4, /device:TPU:1, one launch (start us, length us, event | category | flops | bytes accessed | tf_op | source)
XLA Modules:
  0.0 39.0 jit_solution(2905425020040588255)
XLA Ops:
  0.6 37.5 %lanczos_step.1 = (f32[8,256]{1,0:T(8,128)S(1)}, f32[8,256]{1,0:T(8,128)S(1)}, f32[8,256]{1,0:T(8,128)S(1)}, f32[8,256]{1,0:T(8,128)S(1)}, f32[8,256]{1,0:T(8,12...) custom-call(f32[4,16,256]{2,1,0:T(8,128)} %conductance.1, ...), custom_call_target="tpu_custom_call" | custom-call | tf_op jit(solution)/shard_map/lanczos_step/pallas_call | solution.py:945
  38.1 0.8 %store.1 = (f32[8,16,256]{2,1,0:T(8,128)}, f32[2,8]{1,0:T(2,128)}) custom-call(f32[8,256]{1,0:T(8,128)S(1)} %get-tuple-element.19.refs_0_, f32[8,256]{1,0:T(8,128)S(1)} %get-tuple-element.20.refs_1_, f32[8,256]{1,0:T(8,128)S(1)} %get-tuple-element.21.refs_2_, f32[8,256]{1,0:T(8,128)S(1)} %get-tuple-element.22.refs_3_, ...), custom_call_target="tpu_custom_call" | custom-call | tf_op jit(solution)/shard_map/store/pallas_call | solution.py:974

commit v5 on v4

--- a/solution.py
+++ b/solution.py
@@ -602,6 +602,9 @@
 
 
 def total(x):
+    while x.shape[0] > SUB:
+        half = x.shape[0] // 2
+        x = x[:half] + x[half:]
     return jnp.sum(jnp.sum(x, axis=0, keepdims=True), axis=1, keepdims=True)
 
 

time: 39.1 us -> 39.1 us (level)
  no operation moved by 1% of the time
where the time goes in v5:
time: 39.1 us; the launch traced here: 39 us
  Pallas kernels  38.3 us (98%)
  between operations  0.64 us (2%)
    pallas_call x1, Pallas kernels, local(): pl.pallas_call(step_kernel, out_shape=(shape(SUB, COLS),) * PIECES + (sha...  37.5 us
    pallas_call x1, Pallas kernels, local(): pl.pallas_call(store_kernel, out_shape=(shape(8, ROWS, COLS), shape(2, 8)...  0.82 us

profile of v5, /device:TPU:1, one launch (start us, length us, event | category | flops | bytes accessed | tf_op | source)
XLA Modules:
  0.0 39.0 jit_solution(4295658232678326569)
XLA Ops:
  0.6 37.5 %lanczos_step.1 = (f32[8,256]{1,0:T(8,128)S(1)}, f32[8,256]{1,0:T(8,128)S(1)}, f32[8,256]{1,0:T(8,128)S(1)}, f32[8,256]{1,0:T(8,128)S(1)}, f32[8,256]{1,0:T(8,12...) custom-call(f32[4,16,256]{2,1,0:T(8,128)} %conductance.1, ...), custom_call_target="tpu_custom_call" | custom-call | tf_op jit(solution)/shard_map/lanczos_step/pallas_call | solution.py:948
  38.1 0.8 %store.1 = (f32[8,16,256]{2,1,0:T(8,128)}, f32[2,8]{1,0:T(2,128)}) custom-call(f32[8,256]{1,0:T(8,128)S(1)} %get-tuple-element.19.refs_0_, f32[8,256]{1,0:T(8,128)S(1)} %get-tuple-element.20.refs_1_, f32[8,256]{1,0:T(8,128)S(1)} %get-tuple-element.21.refs_2_, f32[8,256]{1,0:T(8,128)S(1)} %get-tuple-element.22.refs_3_, ...), custom_call_target="tpu_custom_call" | custom-call | tf_op jit(solution)/shard_map/store/pallas_call | solution.py:977
